TPU v7x, 32 devices: a whole 2x2x4 slice. The times are simulated.
32 devices in a mesh: parts: 2 (over y), term: 16 (over z, x, core).
Axes of the slice: x: 2, y: 2, z: 4, core: 2. Of those that a mesh axis runs over, the one named last changes fastest.
Arguments:
- wavefunction: bfloat16 [4096, 1024], P(('parts', 'term')), parts along dimension 0, may hold values from -6 to 6
- left_ops: bfloat16 [320, 512, 512], P(('parts', 'term')), parts along dimension 0, may hold values from -0.0390625 to 0.0390625
- right_ops: bfloat16 [320, 512, 512], P(('parts', 'term')), parts along dimension 0, may hold values from -0.25 to 0.25
- src_sector: int32 [320], P(('parts', 'term')), parts along dimension 0, may hold values from 0 to 3
- dst_sector: int32 [320], P(('parts', 'term')), parts along dimension 0, may hold values from 0 to 3
- live_terms: int32 [32], P(('parts', 'term')), parts along dimension 0, may hold values from 1 to 10, 96 in all
Outputs:
- sigma_pair: float32 [4096, 1024], P(('parts', 'term')), parts along dimension 0
There are 2 independent parts, one for each index of `parts`. A program takes and returns all parts, laid end to end along the dimension named above; each array names one. Nothing has to cross between parts.
Inputs may be any that keep to these rules, and one draw needn't show every extreme that they name: Slots 0 to live_terms[g] - 1 of group g are live; the counts of one part sum to 96 and one group has all 10 live.
All inputs are finite; a program needn't handle non-finite values.
Results may differ from a plain program's by a relative error of at most 0.0029.
Values may be sent and summed in bfloat16 or wider, within the bound.
No kernel may reach another device: no remote copies, remote signals or barrier semaphores. Data moves between devices by JAX's collectives and lax.ppermute only.
A program may use at most 128 MiB of HBM per device.

v0:
```python
import jax
import jax.numpy as jnp
from jax import lax
from jax.sharding import PartitionSpec as P


def term_product(partial_value, left, right, source_id, target_id, source):
    block_width = left.shape[0]
    vec_count = source.shape[1] // block_width
    src_block = lax.dynamic_slice_in_dim(source, source_id * block_width, block_width, 0)
    left_mixed = jnp.dot(left, src_block, preferred_element_type=jnp.float32).astype(jnp.bfloat16)
    stacked = left_mixed.reshape(block_width * vec_count, block_width)
    result = lax.dot_general(
        stacked, right, (((1,), (1,)), ((), ())), preferred_element_type=jnp.float32
    )
    result = result.reshape(block_width, vec_count * block_width)
    row_start = target_id * block_width
    current = lax.dynamic_slice_in_dim(partial_value, row_start, block_width, 0)
    return lax.dynamic_update_slice_in_dim(partial_value, current + result, row_start, 0)


def run_slots(
    partial_value, left_stack, right_stack, source_ids, target_ids, first_slot, stop_slot, source
):

    def add_slot(slot_index, running):
        return term_product(
            running,
            left_stack[slot_index],
            right_stack[slot_index],
            source_ids[slot_index],
            target_ids[slot_index],
            source,
        )

    return lax.fori_loop(first_slot, stop_slot, add_slot, partial_value)


def local(wavefunction, left_ops, right_ops, src_sector, dst_sector, live_terms):
    source = lax.all_gather(wavefunction, "term", axis=0, tiled=True)
    live_count = live_terms[0]
    work_list = (left_ops, right_ops, src_sector, dst_sector, jnp.int32(0), live_count)
    partial_value = jnp.zeros((source.shape[0], source.shape[1]), jnp.float32)
    partial_value = run_slots(
        partial_value,
        work_list[0],
        work_list[1],
        work_list[2],
        work_list[3],
        work_list[4],
        work_list[5],
        source,
    )
    return lax.psum_scatter(partial_value, "term", scatter_dimension=0, tiled=True)


def solution(mesh):
    return jax.shard_map(
        local,
        mesh=mesh,
        in_specs=(
            P(("parts", "term"), None),
            P(("parts", "term"), None, None),
            P(("parts", "term"), None, None),
            P(("parts", "term")),
            P(("parts", "term")),
            P(("parts", "term")),
        ),
        out_specs=P(("parts", "term"), None),
        check_vma=False,
    )
```

profile of v0, /device:TPU:13, one launch (start us, length us, event | category | flops | bytes accessed | tf_op | source)
XLA Modules:
  0.0 319.1 jit_solution(10912474129177407991)
XLA Ops:
  6.5 0.0 copy-start
  6.5 0.0 copy-start.1
  6.5 0.0 all-gather.2.cloned.1.call-start
  6.5 0.7 all-gather.2.cloned.1.call-update
  7.3 0.0 reduce-scatter.2.cloned.1.call-start
  7.3 54.4 %all-gather.2.cloned.1.call-done = bf16[2048,1024]{1,0:T(8,128)(2,1)} async-done(((bf16[128,1024]{1,0:T(8,128)(2,1)}), bf16[2048,1024]{1,0:T(8,128)(2,1)}) %all-gather.2.cloned.1.call-update) | async-done | bytes 4194320 | tf_op jit(solution)/shard_map/all_gather | solution.py:40
  61.7 4.3 %broadcast_in_dim.3 = f32[2048,1024]{1,0:T(8,128)} broadcast(f32[]{:T(128)} %constant.15.clone.1), dimensions={} | broadcast | bytes 8388612 | tf_op jit(solution)/shard_map/broadcast_in_dim | solution.py:43
  66.0 0.0 copy-done
  66.0 0.0 copy-done.1
  66.0 86.2 %while.10 = (s32[]{:T(128)}, f32[2048,1024]{1,0:T(8,128)}, s32[]{:T(128)}, s32[10]{0:T(128)S(1)}, bf16[10,512,512]{2,1,0:T(8,128)(2,1)}, /*index=5*/s32[10]{0:T(...) while((s32[]{:T(128)}, f32[2048,1024]{1,0:T(8,128)}, ...), condition=%wide.region_1.0_spmd, body=%wide.region_0.0_spmd.sunk | while | flops 1074790400 | bytes 18874668 | solution.py:36
  66.6 0.7 dynamic_slice.39
  68.0 0.7 dynamic_slice.40
  69.3 2.1 convolution_convert_fusion.2
  71.4 0.4 reshape.12
  71.8 3.1 fusion.18
  75.0 1.9 reshape.13
  76.9 3.3 %add_dynamic-update-slice_fusion.2 = f32[2048,1024]{1,0:T(8,128)} fusion(f32[2048,1024]{1,0:T(8,128)} %get-tuple-element.129, s32[]{:T(128)S(6)} %select_n.17, f32[512,1024]{1,0:T(8,128)S(1)} %reshape.13), kind=kLoop, calls=%fused_computation.clone.1 | loop fusion | flops 524288 | bytes 6291460 | tf_op jit(solution)/shard_map/while/body/dynamic_update_slice | solution.py:19
  80.9 0.7 dynamic_slice.39
  82.3 0.7 dynamic_slice.40
  83.6 2.1 convolution_convert_fusion.2
  85.7 0.4 reshape.12
  86.1 3.1 fusion.18
  89.2 1.9 reshape.13
  91.2 3.3 %add_dynamic-update-slice_fusion.2 = f32[2048,1024]{1,0:T(8,128)} fusion(f32[2048,1024]{1,0:T(8,128)} %get-tuple-element.129, s32[]{:T(128)S(6)} %select_n.17, f32[512,1024]{1,0:T(8,128)S(1)} %reshape.13), kind=kLoop, calls=%fused_computation.clone.1 | loop fusion | flops 524288 | bytes 6291460 | tf_op jit(solution)/shard_map/while/body/dynamic_update_slice | solution.py:19
  95.2 0.7 dynamic_slice.39
  96.5 0.7 dynamic_slice.40
  97.9 2.1 convolution_convert_fusion.2
  100.0 0.4 reshape.12
  100.4 3.1 fusion.18
  103.5 1.9 reshape.13
  105.5 3.3 %add_dynamic-update-slice_fusion.2 = f32[2048,1024]{1,0:T(8,128)} fusion(f32[2048,1024]{1,0:T(8,128)} %get-tuple-element.129, s32[]{:T(128)S(6)} %select_n.17, f32[512,1024]{1,0:T(8,128)S(1)} %reshape.13), kind=kLoop, calls=%fused_computation.clone.1 | loop fusion | flops 524288 | bytes 6291460 | tf_op jit(solution)/shard_map/while/body/dynamic_update_slice | solution.py:19
  109.5 0.7 dynamic_slice.39
  110.8 0.7 dynamic_slice.40
  112.2 2.1 convolution_convert_fusion.2
  114.3 0.4 reshape.12
  114.7 3.1 fusion.18
  117.8 1.9 reshape.13
  119.7 3.3 %add_dynamic-update-slice_fusion.2 = f32[2048,1024]{1,0:T(8,128)} fusion(f32[2048,1024]{1,0:T(8,128)} %get-tuple-element.129, s32[]{:T(128)S(6)} %select_n.17, f32[512,1024]{1,0:T(8,128)S(1)} %reshape.13), kind=kLoop, calls=%fused_computation.clone.1 | loop fusion | flops 524288 | bytes 6291460 | tf_op jit(solution)/shard_map/while/body/dynamic_update_slice | solution.py:19
  123.7 0.7 dynamic_slice.39
  125.1 0.7 dynamic_slice.40
  126.4 2.1 convolution_convert_fusion.2
  128.5 0.4 reshape.12
  128.9 3.1 fusion.18
  132.1 1.9 reshape.13
  134.0 3.3 %add_dynamic-update-slice_fusion.2 = f32[2048,1024]{1,0:T(8,128)} fusion(f32[2048,1024]{1,0:T(8,128)} %get-tuple-element.129, s32[]{:T(128)S(6)} %select_n.17, f32[512,1024]{1,0:T(8,128)S(1)} %reshape.13), kind=kLoop, calls=%fused_computation.clone.1 | loop fusion | flops 524288 | bytes 6291460 | tf_op jit(solution)/shard_map/while/body/dynamic_update_slice | solution.py:19
  138.0 0.7 dynamic_slice.39
  139.3 0.7 dynamic_slice.40
  140.7 2.1 convolution_convert_fusion.2
  142.8 0.4 reshape.12
  143.2 3.1 fusion.18
  146.3 1.9 reshape.13
  148.2 3.3 %add_dynamic-update-slice_fusion.2 = f32[2048,1024]{1,0:T(8,128)} fusion(f32[2048,1024]{1,0:T(8,128)} %get-tuple-element.129, s32[]{:T(128)S(6)} %select_n.17, f32[512,1024]{1,0:T(8,128)S(1)} %reshape.13), kind=kLoop, calls=%fused_computation.clone.1 | loop fusion | flops 524288 | bytes 6291460 | tf_op jit(solution)/shard_map/while/body/dynamic_update_slice | solution.py:19
  152.2 0.0 reduce-scatter.2.cloned.1.call-update
  152.2 160.0 %reduce-scatter.2.cloned.1.call-done = f32[128,1024]{1,0:T(8,128)} async-done(((f32[2048,1024]{1,0:T(8,128)}), f32[128,1024]{1,0:T(8,128)}) %reduce-scatter.2.cloned.1.call-update) | async-done | bytes 524304 | tf_op jit(solution)/shard_map/reduce_scatter | solution.py:54
Async XLA Ops:
  6.5 59.4 %copy-start = (s32[10]{0:T(128)S(1)}, s32[10]{0:T(128)}, u32[]{:S(2)}) copy-start(s32[10]{0:T(128)} %param.12) | copy-start | bytes 124
  6.5 59.4 %copy-start.1 = (s32[10]{0:T(128)S(1)}, s32[10]{0:T(128)}, u32[]{:S(2)}) copy-start(s32[10]{0:T(128)} %param.11) | copy-start | bytes 124
  6.5 55.1 %all-gather.2.cloned.1.call-start = ((), (), s32[]{:S(2)}) async-start(), calls=%async_computation.1 | async-start | bytes 4456448 | tf_op jit(solution)/shard_map/all_gather | solution.py:40
  7.3 305.0 %reduce-scatter.2.cloned.1.call-start = ((), (), s32[]{:S(2)}) async-start(), calls=%async_computation.2 | async-start | bytes 8912896 | tf_op jit(solution)/shard_map/reduce_scatter | solution.py:54
Sparse Core Ops, SparseCore 0:
  9.5 52.0 all-gather.1
  152.4 159.8 reduce-scatter.1
where the time goes:
time: 322 us; the launch traced here: 319 us
  waiting for transfers between devices  215 us (67%)
  matrix products  31.4 us (10%)
  local copies, waits for them, and re-layouts  26.1 us (8%)
  other arithmetic  20 us (6%)
  between operations  13.4 us (4%)
  loops' own time  13.1 us (4%)
    reduce_scatter x1, waiting for transfers between devices, local(): lax.psum_scatter(partial_value, 'term', scatter_dimension=0, tiled=True)  160 us
    all_gather x1, waiting for transfers between devices, local(): source = lax.all_gather(wavefunction, 'term', axis=0, tiled=True)  54.4 us
    dynamic_update_slice x6, other arithmetic, term_product(): lax.dynamic_update_slice_in_dim(partial_value, current + result, row_star...  20 us
    dot_general x6, matrix products, term_product(): lax.dot_general(stacked, right, (((1,), (1,)), ((), ())), preferred_eleme...  18.7 us
    another operation x1, loops' own time, run_slots(): return lax.fori_loop(first_slot, stop_slot, add_slot, partial_value)  13.1 us
    dot_general x6, matrix products, term_product(): jnp.dot(left, src_block, preferred_element_type=jnp.float32)  12.6 us
    reshape x6, local copies, waits for them, and re-layouts, term_product(): result = result.reshape(block_width, vec_count * block_width)  11.6 us
  transfers between devices with their start and end apart: 2, of which 2 were waited for; matrix products, arithmetic and copies ran while one was open for 0% of the time, Pallas kernels for 0%

commit v1 on v0

v1 whole, which is shorter than its diff:
```python
import functools

import jax
import jax.numpy as jnp
from jax import lax
from jax.experimental import pallas as pl
from jax.experimental.pallas import tpu as pltpu
from jax.sharding import PartitionSpec as P

F32, BF16 = jnp.float32, jnp.bfloat16
CORES = 2
VMEM = 48 * 1024 * 1024
ANY = pl.BlockSpec(memory_space=pl.ANY)
SMEM = pl.BlockSpec(memory_space=pltpu.SMEM)
WHOLE = pl.BlockSpec(memory_space=pltpu.VMEM)


def list_slots(own, sib, field, sector, slots, found):
    def look(t, count):
        found[count] = t
        hit = jnp.logical_and(t < own[2 * slots], own[field * slots + t] == sector)
        count = count + hit.astype(jnp.int32)
        found[count] = t + slots
        hit = jnp.logical_and(t < sib[2 * slots], sib[field * slots + t] == sector)
        return count + hit.astype(jnp.int32)

    return lax.fori_loop(0, slots, look, jnp.int32(0))


def start_fetch(term, slots, own_hbm, sib_hbm, target, sem):
    @pl.when(term < slots)
    def _():
        pltpu.make_async_copy(own_hbm.at[term], target, sem).start()

    @pl.when(term >= slots)
    def _():
        pltpu.make_async_copy(sib_hbm.at[term - slots], target, sem).start()


def left_kernel(phase, *refs):
    (own, sib, where, here, others, left, left_sib), refs = refs[:7], refs[7:]
    mixed, found, source, lbuf, obuf, psem, lsem, osem = refs[-8:]
    slots, depth = left.shape[0], lbuf.shape[0]
    half = here.shape[1]
    bands = others.shape[0] + 1
    sector, band, core = where[phase], where[where.shape[0] - 2], where[where.shape[0] - 1]
    count = list_slots(own, sib, 0, sector, slots, found)
    copies = []
    for j in range(bands):
        b = lax.rem(band + j, bands)
        for i in range(CORES):
            c = core if i == 0 else 1 - core
            row = pl.multiple_of((b * CORES + c) * half, half)
            part = here.at[i] if j == 0 else others.at[j - 1, i]
            copies.append(pltpu.make_async_copy(part, source.at[pl.ds(row, half)], psem.at[j * CORES + i]))
    for copy in copies:
        copy.start()
    for i in range(depth - 1):
        @pl.when(i < count)
        def _():
            start_fetch(found[i], slots, left, left_sib, lbuf.at[i], lsem.at[i])
    for copy in copies:
        copy.wait()

    def out_copy(i):
        return pltpu.make_async_copy(obuf.at[lax.rem(i, 2)], mixed.at[found[i]], osem.at[lax.rem(i, 2)])

    def step(i, carry):
        ahead = i + depth - 1
        @pl.when(ahead < count)
        def _():
            k = lax.rem(ahead, depth)
            start_fetch(found[ahead], slots, left, left_sib, lbuf.at[k], lsem.at[k])

        k = lax.rem(i, depth)
        pltpu.make_async_copy(left.at[0], lbuf.at[k], lsem.at[k]).wait()

        @pl.when(i >= 2)
        def _():
            out_copy(i - 2).wait()

        obuf[lax.rem(i, 2)] = jnp.dot(lbuf[k], source[...], preferred_element_type=F32).astype(BF16)
        out_copy(i).start()
        return carry

    lax.fori_loop(0, count, step, 0)
    for back in (2, 1):
        @pl.when(count >= back)
        def _():
            out_copy(count - back).wait()


def right_kernel(phase, *refs):
    own, sib, where, mixed, right, right_sib, keep, send, found, acc, mbuf, rbuf, msem, rsem = refs
    slots, depth = right.shape[0], rbuf.shape[0]
    half = keep.shape[1]
    bands = send.shape[0] + 1
    sector, band, core = where[phase], where[where.shape[0] - 2], where[where.shape[0] - 1]
    count = list_slots(own, sib, 1, sector, slots, found)

    def fetch(i, k):
        term = found[i]
        pltpu.make_async_copy(mixed.at[term], mbuf.at[k], msem.at[k]).start()
        start_fetch(term, slots, right, right_sib, rbuf.at[k], rsem.at[k])

    for i in range(depth - 1):
        @pl.when(i < count)
        def _():
            fetch(i, i)
    acc[...] = jnp.zeros_like(acc)

    def step(i, carry):
        ahead = i + depth - 1
        @pl.when(ahead < count)
        def _():
            fetch(ahead, lax.rem(ahead, depth))

        k = lax.rem(i, depth)
        pltpu.make_async_copy(mixed.at[0], mbuf.at[k], msem.at[k]).wait()
        pltpu.make_async_copy(right.at[0], rbuf.at[k], rsem.at[k]).wait()
        acc[...] += lax.dot_general(mbuf[k], rbuf[k], (((1,), (1,)), ((), ())), preferred_element_type=F32)
        return carry

    lax.fori_loop(0, count, step, 0)
    for j in range(bands):
        b = lax.rem(band + j, bands)
        for i in range(CORES):
            c = core if i == 0 else 1 - core
            rows = acc[pl.ds(pl.multiple_of((b * CORES + c) * half, half), half)]
            if j == 0:
                keep[i] = rows
            else:
                send[j - 1, i] = rows.astype(BF16)


def local(devices, wavefunction, left, right, src, dst, live):
    slots, width = left.shape[0], left.shape[1]
    half = wavefunction.shape[0]
    sectors = half * devices // width
    bands = devices // (sectors * CORES)
    me = lax.axis_index("term")
    core, band, plane = me % CORES, (me // CORES) % bands, me // (CORES * bands)

    def shift(value, planes=0, band_step=0, flip=False):
        pairs = []
        for i in range(devices):
            c, b, a = i % CORES, (i // CORES) % bands, i // (CORES * bands)
            c = 1 - c if flip else c
            b, a = (b + band_step) % bands, (a + planes) % sectors
            pairs.append((i, (a * bands + b) * CORES + c))
        return lax.ppermute(value, "term", pairs)

    def bands_of(block):
        return jnp.stack([shift(block, band_step=-j) for j in range(1, bands)])

    own_meta = jnp.concatenate([src, dst, live])
    sib_meta = shift(own_meta, flip=True)
    columns = wavefunction.reshape(half, CORES, width)
    mine = lax.dynamic_index_in_dim(columns, core, 1, keepdims=False)
    theirs = lax.dynamic_index_in_dim(columns, 1 - core, 1, keepdims=False)
    chip_block = jnp.stack([mine, shift(theirs, flip=True)])
    left_sib = shift(left, flip=True)
    right_sib = shift(right, flip=True)

    src_order = [0, 1, 3, 2][:sectors] if sectors == 4 else list(range(sectors))
    dst_order = [2, 1, 3, 0] if sectors == 4 else list(range(1, sectors)) + [0]
    blocks = [shift(chip_block, planes=d) if d else chip_block for d in src_order]
    where_src = jnp.stack([(plane - d) % sectors for d in src_order] + [band, core]).astype(jnp.int32)
    where_dst = jnp.stack([(plane + d) % sectors for d in dst_order] + [band, core]).astype(jnp.int32)

    params = pltpu.CompilerParams(vmem_limit_bytes=VMEM)
    term_flops = 2 * width**3
    depth = 4
    mixed = None
    for phase in range(sectors):
        operands = [own_meta, sib_meta, where_src, blocks[phase], bands_of(blocks[phase]), left, left_sib]
        if mixed is not None:
            operands.append(mixed)
        mixed = pl.pallas_call(
            functools.partial(left_kernel, phase),
            out_shape=jax.ShapeDtypeStruct((CORES * slots, width, width), BF16),
            in_specs=[SMEM] * 3 + [ANY] * (len(operands) - 3),
            out_specs=ANY,
            scratch_shapes=[
                pltpu.SMEM((CORES * slots + 1,), jnp.int32),
                pltpu.VMEM((width, width), BF16),
                pltpu.VMEM((depth, width, width), BF16),
                pltpu.VMEM((2, width, width), BF16),
                pltpu.SemaphoreType.DMA((bands * CORES,)),
                pltpu.SemaphoreType.DMA((depth,)),
                pltpu.SemaphoreType.DMA((2,)),
            ],
            input_output_aliases={} if mixed is None else {7: 0},
            compiler_params=params,
            cost_estimate=pl.CostEstimate(flops=3 * term_flops, bytes_accessed=7 * width * width * 2, transcendentals=0),
            name="left_mix",
        )(*operands)

    totals = []
    for phase in range(sectors):
        d = dst_order[phase]
        keep, send = pl.pallas_call(
            functools.partial(right_kernel, phase),
            out_shape=(
                jax.ShapeDtypeStruct((CORES, half, width), F32),
                jax.ShapeDtypeStruct((bands - 1, CORES, half, width), BF16),
            ),
            in_specs=[SMEM] * 3 + [ANY] * 3,
            out_specs=(WHOLE, WHOLE),
            scratch_shapes=[
                pltpu.SMEM((CORES * slots + 1,), jnp.int32),
                pltpu.VMEM((width, width), F32),
                pltpu.VMEM((depth, width, width), BF16),
                pltpu.VMEM((depth, width, width), BF16),
                pltpu.SemaphoreType.DMA((depth,)),
                pltpu.SemaphoreType.DMA((depth,)),
            ],
            compiler_params=params,
            cost_estimate=pl.CostEstimate(flops=3 * term_flops, bytes_accessed=9 * width * width * 2, transcendentals=0),
            name="right_mix",
        )(own_meta, sib_meta, where_dst, mixed, right, right_sib)
        for j in range(1, bands):
            keep = keep + shift(send[j - 1], band_step=j).astype(F32)
        if d:
            keep = keep.astype(BF16)
            totals.append((shift(keep[0], planes=d), shift(keep[1], planes=d, flip=True)))
        else:
            totals.append((keep[0], shift(keep[1].astype(BF16), flip=True)))
    same = sum(t[0].astype(F32) for t in totals)
    cross = sum(t[1].astype(F32) for t in totals)
    first = core == 0
    return jnp.concatenate([jnp.where(first, same, cross), jnp.where(first, cross, same)], axis=1)


def solution(mesh):
    spec = P(("parts", "term"))
    return jax.shard_map(
        functools.partial(local, mesh.shape["term"]),
        mesh=mesh,
        in_specs=(spec,) * 6,
        out_specs=spec,
        check_vma=False,
    )
```

time: 322 us -> 108 us (0.34); the launches traced: 319 us -> 109 us
  waiting for transfers between devices: 215 us -> 30.9 us
  starting transfers between devices: 0.04 us -> 42.5 us
  matrix products: 31.4 us -> 0 us
  Pallas kernels: 0 us -> 27.6 us
  local copies, waits for them, and re-layouts: 26.1 us -> 4.5 us
  other arithmetic: 20 us -> 2.03 us
  loops' own time: 13.1 us -> 0 us
  between operations: 13.4 us -> 0.98 us
    reduce_scatter x1 -> x0, waiting for transfers between devices: 160 us -> none  [local(): lax.psum_scatter(partial_value, 'term', scatter_dimension=0, tiled=True)]
    all_gather x1 -> x0, waiting for transfers between devices: 54.4 us -> none  [local(): source = lax.all_gather(wavefunction, 'term', axis=0, tiled=True)]
    ppermute x0 -> x22, starting transfers between devices: none -> 42.5 us  [shift(): return lax.ppermute(value, 'term', pairs)]
    dot_general x12 -> x0, matrix products: 31.4 us -> none  [the longest x6 18.7 us: term_product(): lax.dot_general(stacked, right, (((1,), (1,)), ((), ())), preferred_eleme...]
    ppermute x0 -> x22, waiting for transfers between devices: none -> 30.9 us  [shift(): return lax.ppermute(value, 'term', pairs)]
    pallas_call x0 -> x8, Pallas kernels: none -> 27.6 us  [the longest x4 16.1 us: local(): pl.pallas_call(functools.partial(left_kernel, phase), out_shape=jax.Shape...]
    dynamic_update_slice x6 -> x0, other arithmetic: 20 us -> none  [term_product(): lax.dynamic_update_slice_in_dim(partial_value, current + result, row_star...]
    another operation x1 -> x0, loops' own time: 13.1 us -> none  [run_slots(): return lax.fori_loop(first_slot, stop_slot, add_slot, partial_value)]
  transfers between devices with their start and end apart: 2 -> 22, of which waited for: 2 -> 7; matrix products, arithmetic and copies ran while one was open for 0% -> 3% of each run, Pallas kernels for 0% -> 23%
where the time goes in v1:
time: 108 us; the launch traced here: 109 us
  starting transfers between devices  42.5 us (39%)
  waiting for transfers between devices  30.9 us (29%)
  Pallas kernels  27.6 us (26%)
  local copies, waits for them, and re-layouts  4.5 us (4%)
  other arithmetic  2.03 us (2%)
    ppermute x22, starting transfers between devices, shift(): return lax.ppermute(value, 'term', pairs)  42.5 us
    ppermute x22, waiting for transfers between devices, shift(): return lax.ppermute(value, 'term', pairs)  30.9 us
    pallas_call x4, Pallas kernels, local(): pl.pallas_call(functools.partial(left_kernel, phase), out_shape=jax.Shape...  16.1 us
    pallas_call x4, Pallas kernels, local(): pl.pallas_call(functools.partial(right_kernel, phase), out_shape=(jax.Sha...  11.5 us
    unnamed x12, local copies, waits for them, and re-layouts  2.56 us
  transfers between devices with their start and end apart: 22, of which 7 were waited for; matrix products, arithmetic and copies ran while one was open for 3% of the time, Pallas kernels for 23%

profile of v1, /device:TPU:13, one launch (start us, length us, event | category | flops | bytes accessed | tf_op | source)
XLA Modules:
  0.0 108.5 jit_solution(16159882298051094063)
XLA Ops:
  0.0 0.7 collective-permute-start.4
  0.7 0.0 collective-permute-start.10
  0.7 1.1 %reshape.5 = bf16[128,2,512]{2,1,0:T(2,128)(2,1)S(1)} reshape(bf16[128,1024]{1,0:T(8,128)(2,1)} %param.6) | data formatting | bytes 524288 | tf_op jit(solution)/shard_map/reshape | solution.py:158
  1.8 0.0 slice-start
  1.9 0.5 constant_dynamic-slice_fusion.1
  2.4 0.6 collective-permute-start.1
  3.0 6.3 %collective-permute-done.1 = bf16[128,512]{1,0:T(8,128)(2,1)S(1)} collective-permute-done((bf16[128,512]{1,0:T(8,128)(2,1)S(1)}, bf16[128,512]{1,0:T(8,128)(2,1)S(1)}, u32[]{:S(2)}, u32[]{:S(2)}) %collective-permute-start.1) | collective-permute-done | bytes 131104 | tf_op jit(solution)/shard_map/ppermute | solution.py:151
  9.4 1.3 %collective-permute-start.9 = (bf16[2,128,512]{2,1,0:T(8,128)(2,1)S(1)}, bf16[2,128,512]{2,1,0:T(8,128)(2,1)S(1)}, u32[]{:S(2)}, u32[]{:S(2)}) collective-permute-start(bf16[2,128,512]{2,1,0:T(8,128)(2,1)S(1)} %pad_maximum_fusion.1.refs_3_), channel_id=1, source_target_pairs={{0,2},{1,3},{2,0},{3,1},{4,6},{5,7},{6,4},{7,5},{8,10},{9,11},{10,... | collective-permute-start | bytes 786440 | tf_op jit(solution)/shard_map/ppermute | solution.py:151
  11.3 1.3 %collective-permute-start.7 = (bf16[2,128,512]{2,1,0:T(8,128)(2,1)S(1)}, bf16[2,128,512]{2,1,0:T(8,128)(2,1)S(1)}, u32[]{:S(2)}, u32[]{:S(2)}) collective-permute-start(bf16[2,128,512]{2,1,0:T(8,128)(2,1)S(1)} %pad_maximum_fusion.1.refs_3_), channel_id=1, source_target_pairs={{0,4},{1,5},{2,6},{3,7},{4,8},{5,9},{6,10},{7,11},{8,12},{9,13},{1... | collective-permute-start | bytes 786440 | tf_op jit(solution)/shard_map/ppermute | solution.py:151
  12.6 0.7 pad_add_fusion.refs_0_
  13.4 0.9 collective-permute-start
  14.3 2.3 %collective-permute-done.refs_1_ = s32[21]{0:T(128)S(1)} collective-permute-done((s32[21]{0:T(128)S(1)}, s32[21]{0:T(128)S(1)}, u32[]{:S(2)}, u32[]{:S(2)}) %collective-permute-start) | collective-permute-done | bytes 116 | tf_op jit(solution)/shard_map/ppermute | solution.py:151
  16.6 0.2 collective-permute-start.5
  16.8 0.1 collective-permute-done.9
  17.0 2.3 %collective-permute-start.2 = (bf16[2,128,512]{2,1,0:T(8,128)(2,1)S(1)}, bf16[2,128,512]{2,1,0:T(8,128)(2,1)S(1)}, u32[]{:S(2)}, u32[]{:S(2)}) collective-permute-start(bf16[2,128,512]{2,1,0:T(8,128)(2,1)S(1)} %pad_maximum_fusion.1.refs_3_), channel_id=1, source_target_pairs={{0,8},{1,9},{2,10},{3,11},{4,12},{5,13},{6,14},{7,15},{8,0},{9,1},... | collective-permute-start | bytes 786440 | tf_op jit(solution)/shard_map/ppermute | solution.py:151
  19.3 0.0 collective-permute-done.7.refs_3_
  19.3 1.2 %collective-permute-start.8 = (bf16[2,128,512]{2,1,0:T(8,128)(2,1)S(1)}, bf16[2,128,512]{2,1,0:T(8,128)(2,1)S(1)}, u32[]{:S(2)}, u32[]{:S(2)}) collective-permute-start(bf16[2,128,512]{2,1,0:T(8,128)(2,1)S(1)} %collective-permute-done.7.refs_3_), channel_id=1, source_target_pairs={{0,2},{1,3},{2,0},{3,1},{4,6},{5,7},{6,4},{7,5},{8,10},{9,11},{10,... | collective-permute-start | bytes 786440 | tf_op jit(solution)/shard_map/ppermute | solution.py:151
  20.5 6.1 %collective-permute-done.5.refs_3_ = bf16[2,128,512]{2,1,0:T(8,128)(2,1)S(1)} collective-permute-done((bf16[2,128,512]{2,1,0:T(8,128)(2,1)S(1)}, bf16[2,128,512]{2,1,0:T(8,128)(2,1)S(1)}, u32[]{:S(2)}, u32[]{:S(2)}) %collective-permute-start.5) | collective-permute-done | bytes 262176 | tf_op jit(solution)/shard_map/ppermute | solution.py:151
  26.6 0.0 collective-permute-start.6
  26.6 9.3 %collective-permute-done.2.refs_3_ = bf16[2,128,512]{2,1,0:T(8,128)(2,1)S(1)} collective-permute-done((bf16[2,128,512]{2,1,0:T(8,128)(2,1)S(1)}, bf16[2,128,512]{2,1,0:T(8,128)(2,1)S(1)}, u32[]{:S(2)}, u32[]{:S(2)}) %collective-permute-start.2) | collective-permute-done | bytes 262176 | tf_op jit(solution)/shard_map/ppermute | solution.py:151
  35.9 1.2 %collective-permute-start.3 = (bf16[2,128,512]{2,1,0:T(8,128)(2,1)S(1)}, bf16[2,128,512]{2,1,0:T(8,128)(2,1)S(1)}, u32[]{:S(2)}, u32[]{:S(2)}) collective-permute-start(bf16[2,128,512]{2,1,0:T(8,128)(2,1)S(1)} %collective-permute-done.2.refs_3_), channel_id=1, source_target_pairs={{0,2},{1,3},{2,0},{3,1},{4,6},{5,7},{6,4},{7,5},{8,10},{9,11},{10,... | collective-permute-start | bytes 786440 | tf_op jit(solution)/shard_map/ppermute | solution.py:151
  37.1 0.1 stack.67.refs_2_
  37.2 0.1 stack.63.refs_2_
  37.2 0.0 collective-permute-done.4.refs_6_
  37.2 2.5 %copy-done = bf16[10,512,512]{2,1,0:T(8,128)(2,1)S(1)} copy-done((bf16[10,512,512]{2,1,0:T(8,128)(2,1)S(1)}, bf16[10,512,512]{2,1,0:T(8,128)(2,1)}, u32[]{:S(2)}) %copy-start) | copy-done | bytes 5242904
  39.7 3.7 %left_mix.4.refs_7_ = bf16[20,512,512]{2,1,0:T(8,128)(2,1)} custom-call(s32[21]{0:T(128)S(1)} %pad_add_fusion.refs_0_, s32[21]{0:T(128)S(1)} %collective-permute-done.refs_1_, s32[6]{0:T(128)S(1)} %stack.67.refs_2_, bf16[2,128,512]{2,1,0:T(8,128)(2,1)S(1)} %pad_maximum_fusion.1.refs_3_, bf16[1,2,128,512]{3,2,1,0:T(8,128)(2,1)S(1)} %bitcast.50, ...), custom_call_target="tpu_custom_call" | custom-call | flops 805306368 | bytes 3670016 | tf_op jit(solution)/shard_map/left_mix/pallas_call | solution.py:179
  43.5 0.0 collective-permute-done.8
  43.5 2.7 %left_mix.5.refs_7_ = bf16[20,512,512]{2,1,0:T(8,128)(2,1)} custom-call(s32[21]{0:T(128)S(1)} %pad_add_fusion.refs_0_, s32[21]{0:T(128)S(1)} %collective-permute-done.refs_1_, s32[6]{0:T(128)S(1)} %stack.67.refs_2_, bf16[2,128,512]{2,1,0:T(8,128)(2,1)S(1)} %collective-permute-done.7.refs_3_, ...), custom_call_target="tpu_custom_call", output_to_operand_aliasing={{}: (7, {})} | custom-call | flops 805306368 | bytes 3670016 | tf_op jit(solution)/shard_map/left_mix/pallas_call | solution.py:179
  46.3 0.0 collective-permute-done.6
  46.3 0.0 slice-start.2
  46.3 4.2 %left_mix.6.refs_7_ = bf16[20,512,512]{2,1,0:T(8,128)(2,1)} custom-call(s32[21]{0:T(128)S(1)} %pad_add_fusion.refs_0_, s32[21]{0:T(128)S(1)} %collective-permute-done.refs_1_, s32[6]{0:T(128)S(1)} %stack.67.refs_2_, bf16[2,128,512]{2,1,0:T(8,128)(2,1)S(1)} %collective-permute-done.5.refs_3_, ...), custom_call_target="tpu_custom_call", output_to_operand_aliasing={{}: (7, {})} | custom-call | flops 805306368 | bytes 3670016 | tf_op jit(solution)/shard_map/left_mix/pallas_call | solution.py:179
  50.5 0.0 slice-start.3
  50.5 0.0 collective-permute-done.3
  50.5 5.4 %left_mix.7.refs_3_ = bf16[20,512,512]{2,1,0:T(8,128)(2,1)} custom-call(s32[21]{0:T(128)S(1)} %pad_add_fusion.refs_0_, s32[21]{0:T(128)S(1)} %collective-permute-done.refs_1_, s32[6]{0:T(128)S(1)} %stack.67.refs_2_, bf16[2,128,512]{2,1,0:T(8,128)(2,1)S(1)} %collective-permute-done.2.refs_3_, ...), custom_call_target="tpu_custom_call", output_to_operand_aliasing={{}: (7, {})} | custom-call | flops 805306368 | bytes 3670016 | tf_op jit(solution)/shard_map/left_mix/pallas_call | solution.py:179
  56.0 0.0 collective-permute-done.10.refs_5_
  56.0 2.3 %right_mix.4 = (f32[2,128,512]{2,1,0:T(8,128)S(1)}, bf16[1,2,128,512]{3,2,1,0:T(8,128)(2,1)S(1)}) custom-call(s32[21]{0:T(128)S(1)} %pad_add_fusion.refs_0_, s32[21]{0:T(128)S(1)} %collective-permute-done.refs_1_, s32[6]{0:T(128)S(1)} %stack.63.refs_2_, bf16[20,512,512]{2,1,0:T(8,128)(2,1)} %left_mix.7.refs_3_, bf16[10,512,512]{2,1,0:T(8,128)(2,1)S(1)} %bitcast.49, ...), custom_call_target="tpu_custom_call" | custom-call | flops 805306368 | bytes 4718592 | tf_op jit(solution)/shard_map/right_mix/pallas_call | solution.py:202
  58.3 0.1 collective-permute-start.11
  58.4 2.5 %right_mix.5 = (f32[2,128,512]{2,1,0:T(8,128)S(1)}, bf16[1,2,128,512]{3,2,1,0:T(8,128)(2,1)S(1)}) custom-call(s32[21]{0:T(128)S(1)} %pad_add_fusion.refs_0_, s32[21]{0:T(128)S(1)} %collective-permute-done.refs_1_, s32[6]{0:T(128)S(1)} %stack.63.refs_2_, bf16[20,512,512]{2,1,0:T(8,128)(2,1)} %left_mix.7.refs_3_, bf16[10,512,512]{2,1,0:T(8,128)(2,1)S(1)} %bitcast.49, ...), custom_call_target="tpu_custom_call" | custom-call | flops 805306368 | bytes 4718592 | tf_op jit(solution)/shard_map/right_mix/pallas_call | solution.py:202
  60.9 1.8 %collective-permute-start.13 = (bf16[2,128,512]{2,1,0:T(8,128)(2,1)S(1)}, bf16[2,128,512]{2,1,0:T(8,128)(2,1)S(1)}, u32[]{:S(2)}, u32[]{:S(2)}) collective-permute-start(bf16[2,128,512]{2,1,0:T(8,128)(2,1)S(1)} %bitcast.56), channel_id=1, source_target_pairs={{0,2},{1,3},{2,0},{3,1},{4,6},{5,7},{6,4},{7,5},{8,10},{9,11},{10,... | collective-permute-start | bytes 786440 | tf_op jit(solution)/shard_map/ppermute | solution.py:151
  62.7 2.5 %right_mix.6 = (f32[2,128,512]{2,1,0:T(8,128)S(1)}, bf16[1,2,128,512]{3,2,1,0:T(8,128)(2,1)S(1)}) custom-call(s32[21]{0:T(128)S(1)} %pad_add_fusion.refs_0_, s32[21]{0:T(128)S(1)} %collective-permute-done.refs_1_, s32[6]{0:T(128)S(1)} %stack.63.refs_2_, bf16[20,512,512]{2,1,0:T(8,128)(2,1)} %left_mix.7.refs_3_, bf16[10,512,512]{2,1,0:T(8,128)(2,1)S(1)} %bitcast.49, ...), custom_call_target="tpu_custom_call" | custom-call | flops 805306368 | bytes 4718592 | tf_op jit(solution)/shard_map/right_mix/pallas_call | solution.py:202
  65.2 0.1 collective-permute-start.15
  65.3 4.2 %right_mix.7 = (f32[2,128,512]{2,1,0:T(8,128)S(1)}, bf16[1,2,128,512]{3,2,1,0:T(8,128)(2,1)S(1)}) custom-call(s32[21]{0:T(128)S(1)} %pad_add_fusion.refs_0_, s32[21]{0:T(128)S(1)} %collective-permute-done.refs_1_, s32[6]{0:T(128)S(1)} %stack.63.refs_2_, bf16[20,512,512]{2,1,0:T(8,128)(2,1)} %left_mix.7.refs_3_, bf16[10,512,512]{2,1,0:T(8,128)(2,1)S(1)} %bitcast.49, ...), custom_call_target="tpu_custom_call" | custom-call | flops 805306368 | bytes 4718592 | tf_op jit(solution)/shard_map/right_mix/pallas_call | solution.py:202
  69.5 0.1 collective-permute-start.17
  69.6 0.0 collective-permute-done.11
  69.6 0.1 add_convert_fusion.2
  69.7 13.5 %collective-permute-start.12 = (bf16[128,512]{1,0:T(8,128)(2,1)S(1)}, bf16[128,512]{1,0:T(8,128)(2,1)S(1)}, u32[]{:S(2)}, u32[]{:S(2)}) collective-permute-start(bf16[128,512]{1,0:T(8,128)(2,1)S(1)} %get-tuple-element.23), channel_id=1, source_target_pairs={{0,8},{1,9},{2,10},{3,11},{4,12},{5,13},{6,14},{7,15},{8,0},{9,1},... | collective-permute-start | bytes 393224 | tf_op jit(solution)/shard_map/ppermute | solution.py:151
  83.2 1.8 %collective-permute-start.18 = (bf16[128,512]{1,0:T(8,128)(2,1)S(1)}, bf16[128,512]{1,0:T(8,128)(2,1)S(1)}, u32[]{:S(2)}, u32[]{:S(2)}) collective-permute-start(bf16[128,512]{1,0:T(8,128)(2,1)S(1)} %get-tuple-element.24), channel_id=1, source_target_pairs={{0,9},{1,8},{2,11},{3,10},{4,13},{5,12},{6,15},{7,14},{8,1},{9,0},... | collective-permute-start | bytes 393224 | tf_op jit(solution)/shard_map/ppermute | solution.py:151
  85.1 0.0 collective-permute-done.13
  85.1 0.1 add_convert_fusion.1
  85.2 1.9 %collective-permute-start.14 = (bf16[128,512]{1,0:T(8,128)(2,1)S(1)}, bf16[128,512]{1,0:T(8,128)(2,1)S(1)}, u32[]{:S(2)}, u32[]{:S(2)}) collective-permute-start(bf16[128,512]{1,0:T(8,128)(2,1)S(1)} %get-tuple-element.25), channel_id=1, source_target_pairs={{0,4},{1,5},{2,6},{3,7},{4,8},{5,9},{6,10},{7,11},{8,12},{9,13},{1... | collective-permute-start | bytes 393224 | tf_op jit(solution)/shard_map/ppermute | solution.py:151
  87.0 0.0 collective-permute-done.15
  87.0 0.3 collective-permute-start.19
  87.3 0.1 add_convert_fusion
  87.4 6.9 %collective-permute-start.16 = (bf16[128,512]{1,0:T(8,128)(2,1)S(1)}, bf16[128,512]{1,0:T(8,128)(2,1)S(1)}, u32[]{:S(2)}, u32[]{:S(2)}) collective-permute-start(bf16[128,512]{1,0:T(8,128)(2,1)S(1)} %get-tuple-element.27), channel_id=1, source_target_pairs={{0,12},{1,13},{2,14},{3,15},{4,0},{5,1},{6,2},{7,3},{8,4},{9,5},{1... | collective-permute-start | bytes 393224 | tf_op jit(solution)/shard_map/ppermute | solution.py:151
  94.3 0.1 convert_add_fusion
  94.4 6.4 %collective-permute-start.20 = (bf16[128,512]{1,0:T(8,128)(2,1)S(1)}, bf16[128,512]{1,0:T(8,128)(2,1)S(1)}, u32[]{:S(2)}, u32[]{:S(2)}) collective-permute-start(bf16[128,512]{1,0:T(8,128)(2,1)S(1)} %get-tuple-element.28), channel_id=1, source_target_pairs={{0,13},{1,12},{2,15},{3,14},{4,1},{5,0},{6,3},{7,2},{8,5},{9,4},{1... | collective-permute-start | bytes 393224 | tf_op jit(solution)/shard_map/ppermute | solution.py:151
  100.8 0.0 collective-permute-start.21
  100.8 0.0 collective-permute-done.14
  100.8 4.3 %collective-permute-done.19 = bf16[128,512]{1,0:T(8,128)(2,1)S(1)} collective-permute-done((bf16[128,512]{1,0:T(8,128)(2,1)S(1)}, bf16[128,512]{1,0:T(8,128)(2,1)S(1)}, u32[]{:S(2)}, u32[]{:S(2)}) %collective-permute-start.19) | collective-permute-done | bytes 131104 | tf_op jit(solution)/shard_map/ppermute | solution.py:151
  105.1 0.0 collective-permute-done.16
  105.1 2.4 %collective-permute-done.20 = bf16[128,512]{1,0:T(8,128)(2,1)S(1)} collective-permute-done((bf16[128,512]{1,0:T(8,128)(2,1)S(1)}, bf16[128,512]{1,0:T(8,128)(2,1)S(1)}, u32[]{:S(2)}, u32[]{:S(2)}) %collective-permute-start.20) | collective-permute-done | bytes 131104 | tf_op jit(solution)/shard_map/ppermute | solution.py:151
  107.5 0.0 collective-permute-done.21
  107.5 0.1 broadcast_select_fusion.1
  107.7 0.8 pad_maximum_fusion
  (18 shorter events, 0.2 us)
Async XLA Ops:
  0.0 37.2 %collective-permute-start.4 = (bf16[10,512,512]{2,1,0:T(8,128)(2,1)}, bf16[10,512,512]{2,1,0:T(8,128)(2,1)}, u32[]{:S(2)}, u32[]{:S(2)}) collective-permute-start(bf16[10,512,512]{2,1,0:T(8,128)(2,1)} %refs_5_.7), channel_id=1, source_target_pairs={{0,1},{1,0},{2,3},{3,2},{4,5},{5,4},{6,7},{7,6},{8,9},{9,8},{10,11... | collective-permute-start | bytes 15728648 | tf_op jit(solution)/shard_map/ppermute | solution.py:151
  0.7 55.3 %collective-permute-start.10 = (bf16[10,512,512]{2,1,0:T(8,128)(2,1)}, bf16[10,512,512]{2,1,0:T(8,128)(2,1)}, u32[]{:S(2)}, u32[]{:S(2)}) collective-permute-start(bf16[10,512,512]{2,1,0:T(8,128)(2,1)} %refs_4_.7), channel_id=1, source_target_pairs={{0,1},{1,0},{2,3},{3,2},{4,5},{5,4},{6,7},{7,6},{8,9},{9,8},{10,11... | collective-permute-start | bytes 15728648 | tf_op jit(solution)/shard_map/ppermute | solution.py:151
  1.8 41.7 %slice-start = ((s8[5242880]{0:T(1024)(128)(4,1)}), s8[1048576]{0:T(1024)(128)(4,1)S(1)}, s32[]{:S(2)}) async-start(s8[5242880]{0:T(1024)(128)(4,1)} %bitcast.46), calls=%async_computation | async-start | bytes 2097152
  2.4 6.9 %collective-permute-start.1 = (bf16[128,512]{1,0:T(8,128)(2,1)S(1)}, bf16[128,512]{1,0:T(8,128)(2,1)S(1)}, u32[]{:S(2)}, u32[]{:S(2)}) collective-permute-start(bf16[128,512]{1,0:T(8,128)(2,1)S(1)} %bitcast.59), channel_id=1, source_target_pairs={{0,1},{1,0},{2,3},{3,2},{4,5},{5,4},{6,7},{7,6},{8,9},{9,8},{10,11... | collective-permute-start | bytes 393224 | tf_op jit(solution)/shard_map/ppermute | solution.py:151
  9.4 7.6 %collective-permute-start.9 = (bf16[2,128,512]{2,1,0:T(8,128)(2,1)S(1)}, bf16[2,128,512]{2,1,0:T(8,128)(2,1)S(1)}, u32[]{:S(2)}, u32[]{:S(2)}) collective-permute-start(bf16[2,128,512]{2,1,0:T(8,128)(2,1)S(1)} %pad_maximum_fusion.1.refs_3_), channel_id=1, source_target_pairs={{0,2},{1,3},{2,0},{3,1},{4,6},{5,7},{6,4},{7,5},{8,10},{9,11},{10,... | collective-permute-start | bytes 786440 | tf_op jit(solution)/shard_map/ppermute | solution.py:151
  11.3 8.0 %collective-permute-start.7 = (bf16[2,128,512]{2,1,0:T(8,128)(2,1)S(1)}, bf16[2,128,512]{2,1,0:T(8,128)(2,1)S(1)}, u32[]{:S(2)}, u32[]{:S(2)}) collective-permute-start(bf16[2,128,512]{2,1,0:T(8,128)(2,1)S(1)} %pad_maximum_fusion.1.refs_3_), channel_id=1, source_target_pairs={{0,4},{1,5},{2,6},{3,7},{4,8},{5,9},{6,10},{7,11},{8,12},{9,13},{1... | collective-permute-start | bytes 786440 | tf_op jit(solution)/shard_map/ppermute | solution.py:151
  13.4 3.3 %collective-permute-start = (s32[21]{0:T(128)S(1)}, s32[21]{0:T(128)S(1)}, u32[]{:S(2)}, u32[]{:S(2)}) collective-permute-start(s32[21]{0:T(128)S(1)} %pad_add_fusion.refs_0_), channel_id=1, source_target_pairs={{0,1},{1,0},{2,3},{3,2},{4,5},{5,4},{6,7},{7,6},{8,9},{9,8},{10,11... | collective-permute-start | bytes 260 | tf_op jit(solution)/shard_map/ppermute | solution.py:151
  16.6 9.9 %collective-permute-start.5 = (bf16[2,128,512]{2,1,0:T(8,128)(2,1)S(1)}, bf16[2,128,512]{2,1,0:T(8,128)(2,1)S(1)}, u32[]{:S(2)}, u32[]{:S(2)}) collective-permute-start(bf16[2,128,512]{2,1,0:T(8,128)(2,1)S(1)} %pad_maximum_fusion.1.refs_3_), channel_id=1, source_target_pairs={{0,12},{1,13},{2,14},{3,15},{4,0},{5,1},{6,2},{7,3},{8,4},{9,5},{1... | collective-permute-start | bytes 786440 | tf_op jit(solution)/shard_map/ppermute | solution.py:151
  17.0 18.9 %collective-permute-start.2 = (bf16[2,128,512]{2,1,0:T(8,128)(2,1)S(1)}, bf16[2,128,512]{2,1,0:T(8,128)(2,1)S(1)}, u32[]{:S(2)}, u32[]{:S(2)}) collective-permute-start(bf16[2,128,512]{2,1,0:T(8,128)(2,1)S(1)} %pad_maximum_fusion.1.refs_3_), channel_id=1, source_target_pairs={{0,8},{1,9},{2,10},{3,11},{4,12},{5,13},{6,14},{7,15},{8,0},{9,1},... | collective-permute-start | bytes 786440 | tf_op jit(solution)/shard_map/ppermute | solution.py:151
  19.3 24.2 %collective-permute-start.8 = (bf16[2,128,512]{2,1,0:T(8,128)(2,1)S(1)}, bf16[2,128,512]{2,1,0:T(8,128)(2,1)S(1)}, u32[]{:S(2)}, u32[]{:S(2)}) collective-permute-start(bf16[2,128,512]{2,1,0:T(8,128)(2,1)S(1)} %collective-permute-done.7.refs_3_), channel_id=1, source_target_pairs={{0,2},{1,3},{2,0},{3,1},{4,6},{5,7},{6,4},{7,5},{8,10},{9,11},{10,... | collective-permute-start | bytes 786440 | tf_op jit(solution)/shard_map/ppermute | solution.py:151
  26.6 19.7 %collective-permute-start.6 = (bf16[2,128,512]{2,1,0:T(8,128)(2,1)S(1)}, bf16[2,128,512]{2,1,0:T(8,128)(2,1)S(1)}, u32[]{:S(2)}, u32[]{:S(2)}) collective-permute-start(bf16[2,128,512]{2,1,0:T(8,128)(2,1)S(1)} %collective-permute-done.5.refs_3_), channel_id=1, source_target_pairs={{0,2},{1,3},{2,0},{3,1},{4,6},{5,7},{6,4},{7,5},{8,10},{9,11},{10,... | collective-permute-start | bytes 786440 | tf_op jit(solution)/shard_map/ppermute | solution.py:151
  35.9 14.7 %collective-permute-start.3 = (bf16[2,128,512]{2,1,0:T(8,128)(2,1)S(1)}, bf16[2,128,512]{2,1,0:T(8,128)(2,1)S(1)}, u32[]{:S(2)}, u32[]{:S(2)}) collective-permute-start(bf16[2,128,512]{2,1,0:T(8,128)(2,1)S(1)} %collective-permute-done.2.refs_3_), channel_id=1, source_target_pairs={{0,2},{1,3},{2,0},{3,1},{4,6},{5,7},{6,4},{7,5},{8,10},{9,11},{10,... | collective-permute-start | bytes 786440 | tf_op jit(solution)/shard_map/ppermute | solution.py:151
  37.2 2.5 %copy-start = (bf16[10,512,512]{2,1,0:T(8,128)(2,1)S(1)}, bf16[10,512,512]{2,1,0:T(8,128)(2,1)}, u32[]{:S(2)}) copy-start(bf16[10,512,512]{2,1,0:T(8,128)(2,1)} %refs_5_.7) | copy-start | bytes 15728644
  39.7 3.8 %slice-start.1 = ((s8[5242880]{0:T(1024)(128)(4,1)}), s8[4194304]{0:T(1024)(128)(4,1)S(1)}, s32[]{:S(2)}) async-start(s8[5242880]{0:T(1024)(128)(4,1)} %bitcast.46), calls=%async_computation.1 | async-start | bytes 8388608
  46.3 9.7 %slice-start.2 = ((s8[5242880]{0:T(1024)(128)(4,1)}), s8[4194304]{0:T(1024)(128)(4,1)S(1)}, s32[]{:S(2)}) async-start(s8[5242880]{0:T(1024)(128)(4,1)} %bitcast.48), calls=%async_computation.2 | async-start | bytes 8388608
  50.5 5.5 %slice-start.3 = ((s8[5242880]{0:T(1024)(128)(4,1)}), s8[1048576]{0:T(1024)(128)(4,1)S(1)}, s32[]{:S(2)}) async-start(s8[5242880]{0:T(1024)(128)(4,1)} %bitcast.48), calls=%async_computation.3 | async-start | bytes 2097152
  58.3 11.3 %collective-permute-start.11 = (bf16[2,128,512]{2,1,0:T(8,128)(2,1)S(1)}, bf16[2,128,512]{2,1,0:T(8,128)(2,1)S(1)}, u32[]{:S(2)}, u32[]{:S(2)}) collective-permute-start(bf16[2,128,512]{2,1,0:T(8,128)(2,1)S(1)} %bitcast.57), channel_id=1, source_target_pairs={{0,2},{1,3},{2,0},{3,1},{4,6},{5,7},{6,4},{7,5},{8,10},{9,11},{10,... | collective-permute-start | bytes 786440 | tf_op jit(solution)/shard_map/ppermute | solution.py:151
  60.9 24.2 %collective-permute-start.13 = (bf16[2,128,512]{2,1,0:T(8,128)(2,1)S(1)}, bf16[2,128,512]{2,1,0:T(8,128)(2,1)S(1)}, u32[]{:S(2)}, u32[]{:S(2)}) collective-permute-start(bf16[2,128,512]{2,1,0:T(8,128)(2,1)S(1)} %bitcast.56), channel_id=1, source_target_pairs={{0,2},{1,3},{2,0},{3,1},{4,6},{5,7},{6,4},{7,5},{8,10},{9,11},{10,... | collective-permute-start | bytes 786440 | tf_op jit(solution)/shard_map/ppermute | solution.py:151
  65.2 21.8 %collective-permute-start.15 = (bf16[2,128,512]{2,1,0:T(8,128)(2,1)S(1)}, bf16[2,128,512]{2,1,0:T(8,128)(2,1)S(1)}, u32[]{:S(2)}, u32[]{:S(2)}) collective-permute-start(bf16[2,128,512]{2,1,0:T(8,128)(2,1)S(1)} %bitcast.55), channel_id=1, source_target_pairs={{0,2},{1,3},{2,0},{3,1},{4,6},{5,7},{6,4},{7,5},{8,10},{9,11},{10,... | collective-permute-start | bytes 786440 | tf_op jit(solution)/shard_map/ppermute | solution.py:151
  69.5 17.9 %collective-permute-start.17 = (bf16[2,128,512]{2,1,0:T(8,128)(2,1)S(1)}, bf16[2,128,512]{2,1,0:T(8,128)(2,1)S(1)}, u32[]{:S(2)}, u32[]{:S(2)}) collective-permute-start(bf16[2,128,512]{2,1,0:T(8,128)(2,1)S(1)} %bitcast.54), channel_id=1, source_target_pairs={{0,2},{1,3},{2,0},{3,1},{4,6},{5,7},{6,4},{7,5},{8,10},{9,11},{10,... | collective-permute-start | bytes 786440 | tf_op jit(solution)/shard_map/ppermute | solution.py:151
  69.7 24.7 %collective-permute-start.12 = (bf16[128,512]{1,0:T(8,128)(2,1)S(1)}, bf16[128,512]{1,0:T(8,128)(2,1)S(1)}, u32[]{:S(2)}, u32[]{:S(2)}) collective-permute-start(bf16[128,512]{1,0:T(8,128)(2,1)S(1)} %get-tuple-element.23), channel_id=1, source_target_pairs={{0,8},{1,9},{2,10},{3,11},{4,12},{5,13},{6,14},{7,15},{8,0},{9,1},... | collective-permute-start | bytes 393224 | tf_op jit(solution)/shard_map/ppermute | solution.py:151
  83.2 17.6 %collective-permute-start.18 = (bf16[128,512]{1,0:T(8,128)(2,1)S(1)}, bf16[128,512]{1,0:T(8,128)(2,1)S(1)}, u32[]{:S(2)}, u32[]{:S(2)}) collective-permute-start(bf16[128,512]{1,0:T(8,128)(2,1)S(1)} %get-tuple-element.24), channel_id=1, source_target_pairs={{0,9},{1,8},{2,11},{3,10},{4,13},{5,12},{6,15},{7,14},{8,1},{9,0},... | collective-permute-start | bytes 393224 | tf_op jit(solution)/shard_map/ppermute | solution.py:151
  85.2 15.7 %collective-permute-start.14 = (bf16[128,512]{1,0:T(8,128)(2,1)S(1)}, bf16[128,512]{1,0:T(8,128)(2,1)S(1)}, u32[]{:S(2)}, u32[]{:S(2)}) collective-permute-start(bf16[128,512]{1,0:T(8,128)(2,1)S(1)} %get-tuple-element.25), channel_id=1, source_target_pairs={{0,4},{1,5},{2,6},{3,7},{4,8},{5,9},{6,10},{7,11},{8,12},{9,13},{1... | collective-permute-start | bytes 393224 | tf_op jit(solution)/shard_map/ppermute | solution.py:151
  87.0 18.0 %collective-permute-start.19 = (bf16[128,512]{1,0:T(8,128)(2,1)S(1)}, bf16[128,512]{1,0:T(8,128)(2,1)S(1)}, u32[]{:S(2)}, u32[]{:S(2)}) collective-permute-start(bf16[128,512]{1,0:T(8,128)(2,1)S(1)} %get-tuple-element.26), channel_id=1, source_target_pairs={{0,5},{1,4},{2,7},{3,6},{4,9},{5,8},{6,11},{7,10},{8,13},{9,12},{1... | collective-permute-start | bytes 393224 | tf_op jit(solution)/shard_map/ppermute | solution.py:151
  87.4 17.7 %collective-permute-start.16 = (bf16[128,512]{1,0:T(8,128)(2,1)S(1)}, bf16[128,512]{1,0:T(8,128)(2,1)S(1)}, u32[]{:S(2)}, u32[]{:S(2)}) collective-permute-start(bf16[128,512]{1,0:T(8,128)(2,1)S(1)} %get-tuple-element.27), channel_id=1, source_target_pairs={{0,12},{1,13},{2,14},{3,15},{4,0},{5,1},{6,2},{7,3},{8,4},{9,5},{1... | collective-permute-start | bytes 393224 | tf_op jit(solution)/shard_map/ppermute | solution.py:151
  94.4 13.1 %collective-permute-start.20 = (bf16[128,512]{1,0:T(8,128)(2,1)S(1)}, bf16[128,512]{1,0:T(8,128)(2,1)S(1)}, u32[]{:S(2)}, u32[]{:S(2)}) collective-permute-start(bf16[128,512]{1,0:T(8,128)(2,1)S(1)} %get-tuple-element.28), channel_id=1, source_target_pairs={{0,13},{1,12},{2,15},{3,14},{4,1},{5,0},{6,3},{7,2},{8,5},{9,4},{1... | collective-permute-start | bytes 393224 | tf_op jit(solution)/shard_map/ppermute | solution.py:151
  100.8 6.7 %collective-permute-start.21 = (bf16[128,512]{1,0:T(8,128)(2,1)S(1)}, bf16[128,512]{1,0:T(8,128)(2,1)S(1)}, u32[]{:S(2)}, u32[]{:S(2)}) collective-permute-start(bf16[128,512]{1,0:T(8,128)(2,1)S(1)} %fusion.1), channel_id=1, source_target_pairs={{0,1},{1,0},{2,3},{3,2},{4,5},{5,4},{6,7},{7,6},{8,9},{9,8},{10,11... | collective-permute-start | bytes 393224 | tf_op jit(solution)/shard_map/ppermute | solution.py:151

commit v2 on v1

--- a/solution.py
+++ b/solution.py
@@ -9,7 +9,7 @@
 
 F32, BF16 = jnp.float32, jnp.bfloat16
 CORES = 2
-VMEM = 48 * 1024 * 1024
+VMEM = 16 * 1024 * 1024
 ANY = pl.BlockSpec(memory_space=pl.ANY)
 SMEM = pl.BlockSpec(memory_space=pltpu.SMEM)
 WHOLE = pl.BlockSpec(memory_space=pltpu.VMEM)
@@ -39,28 +39,22 @@
 
 def left_kernel(phase, *refs):
     (own, sib, where, here, others, left, left_sib), refs = refs[:7], refs[7:]
-    mixed, found, source, lbuf, obuf, psem, lsem, osem = refs[-8:]
+    mixed, found, source, lbuf, obuf, lsem, osem = refs[-7:]
     slots, depth = left.shape[0], lbuf.shape[0]
     half = here.shape[1]
     bands = others.shape[0] + 1
     sector, band, core = where[phase], where[where.shape[0] - 2], where[where.shape[0] - 1]
     count = list_slots(own, sib, 0, sector, slots, found)
-    copies = []
+    for i in range(depth - 1):
+        @pl.when(i < count)
+        def _():
+            start_fetch(found[i], slots, left, left_sib, lbuf.at[i], lsem.at[i])
     for j in range(bands):
         b = lax.rem(band + j, bands)
         for i in range(CORES):
             c = core if i == 0 else 1 - core
             row = pl.multiple_of((b * CORES + c) * half, half)
-            part = here.at[i] if j == 0 else others.at[j - 1, i]
-            copies.append(pltpu.make_async_copy(part, source.at[pl.ds(row, half)], psem.at[j * CORES + i]))
-    for copy in copies:
-        copy.start()
-    for i in range(depth - 1):
-        @pl.when(i < count)
-        def _():
-            start_fetch(found[i], slots, left, left_sib, lbuf.at[i], lsem.at[i])
-    for copy in copies:
-        copy.wait()
+            source[pl.ds(row, half)] = here[i] if j == 0 else others[j - 1, i]
 
     def out_copy(i):
         return pltpu.make_async_copy(obuf.at[lax.rem(i, 2)], mixed.at[found[i]], osem.at[lax.rem(i, 2)])
@@ -138,67 +132,77 @@
     half = wavefunction.shape[0]
     sectors = half * devices // width
     bands = devices // (sectors * CORES)
+    assert sectors == 4
     me = lax.axis_index("term")
     core, band, plane = me % CORES, (me // CORES) % bands, me // (CORES * bands)
 
-    def shift(value, planes=0, band_step=0, flip=False):
+    def move(value, to_plane=lambda a: a, band_step=0, flip=False):
         pairs = []
         for i in range(devices):
             c, b, a = i % CORES, (i // CORES) % bands, i // (CORES * bands)
             c = 1 - c if flip else c
-            b, a = (b + band_step) % bands, (a + planes) % sectors
-            pairs.append((i, (a * bands + b) * CORES + c))
+            pairs.append((i, (to_plane(a) * bands + (b + band_step) % bands) * CORES + c))
         return lax.ppermute(value, "term", pairs)
 
+    def beside(a):
+        return a ^ 1
+
+    def mirror(a):
+        return 3 - a
+
     def bands_of(block):
-        return jnp.stack([shift(block, band_step=-j) for j in range(1, bands)])
+        return jnp.stack([move(block, band_step=-j) for j in range(1, bands)])
 
     own_meta = jnp.concatenate([src, dst, live])
-    sib_meta = shift(own_meta, flip=True)
-    columns = wavefunction.reshape(half, CORES, width)
-    mine = lax.dynamic_index_in_dim(columns, core, 1, keepdims=False)
-    theirs = lax.dynamic_index_in_dim(columns, 1 - core, 1, keepdims=False)
-    chip_block = jnp.stack([mine, shift(theirs, flip=True)])
-    left_sib = shift(left, flip=True)
-    right_sib = shift(right, flip=True)
-
-    src_order = [0, 1, 3, 2][:sectors] if sectors == 4 else list(range(sectors))
-    dst_order = [2, 1, 3, 0] if sectors == 4 else list(range(1, sectors)) + [0]
-    blocks = [shift(chip_block, planes=d) if d else chip_block for d in src_order]
-    where_src = jnp.stack([(plane - d) % sectors for d in src_order] + [band, core]).astype(jnp.int32)
-    where_dst = jnp.stack([(plane + d) % sectors for d in dst_order] + [band, core]).astype(jnp.int32)
+    sib_meta = move(own_meta, flip=True)
+    mine = lax.dynamic_slice_in_dim(wavefunction, core * width, width, 1)
+    theirs = lax.dynamic_slice_in_dim(wavefunction, (1 - core) * width, width, 1)
+    from_sib = move(theirs, flip=True)
+    left_sib, from_sib = lax.optimization_barrier((left, from_sib))
+    left_sib = move(left_sib, flip=True)
+    own_block = jnp.stack([mine, from_sib])
+    mirror_block = move(own_block, mirror)
+    beside_block = move(own_block, beside)
+    right_sib, mirror_block = lax.optimization_barrier((right, mirror_block))
+    right_sib = move(right_sib, flip=True)
+    blocks = [own_block, beside_block, mirror_block, None]
+    partner = plane ^ 1
+    where_src = jnp.stack([plane, partner, 3 - plane, 3 - partner, band, core]).astype(jnp.int32)
+    where_dst = jnp.stack([3 - partner, 3 - plane, partner, plane, band, core]).astype(jnp.int32)
 
     params = pltpu.CompilerParams(vmem_limit_bytes=VMEM)
-    term_flops = 2 * width**3
+    cost = pl.CostEstimate(flops=4 * 10**9, bytes_accessed=7 * width * width * 2, transcendentals=0)
     depth = 4
     mixed = None
     for phase in range(sectors):
+        if phase == 1:
+            forward, mixed = lax.optimization_barrier((mirror_block, mixed))
+            blocks[3] = move(forward, beside)
+        if phase == 2:
+            blocks[3], mixed = lax.optimization_barrier((blocks[3], mixed))
         operands = [own_meta, sib_meta, where_src, blocks[phase], bands_of(blocks[phase]), left, left_sib]
         if mixed is not None:
             operands.append(mixed)
         mixed = pl.pallas_call(
             functools.partial(left_kernel, phase),
             out_shape=jax.ShapeDtypeStruct((CORES * slots, width, width), BF16),
-            in_specs=[SMEM] * 3 + [ANY] * (len(operands) - 3),
+            in_specs=[SMEM] * 3 + [WHOLE] * 2 + [ANY] * (len(operands) - 5),
             out_specs=ANY,
             scratch_shapes=[
                 pltpu.SMEM((CORES * slots + 1,), jnp.int32),
                 pltpu.VMEM((width, width), BF16),
                 pltpu.VMEM((depth, width, width), BF16),
                 pltpu.VMEM((2, width, width), BF16),
-                pltpu.SemaphoreType.DMA((bands * CORES,)),
                 pltpu.SemaphoreType.DMA((depth,)),
                 pltpu.SemaphoreType.DMA((2,)),
             ],
             input_output_aliases={} if mixed is None else {7: 0},
             compiler_params=params,
-            cost_estimate=pl.CostEstimate(flops=3 * term_flops, bytes_accessed=7 * width * width * 2, transcendentals=0),
+            cost_estimate=cost,
             name="left_mix",
         )(*operands)
 
-    totals = []
-    for phase in range(sectors):
-        d = dst_order[phase]
+    def right_mix(phase, meta):
         keep, send = pl.pallas_call(
             functools.partial(right_kernel, phase),
             out_shape=(
@@ -216,18 +220,20 @@
                 pltpu.SemaphoreType.DMA((depth,)),
             ],
             compiler_params=params,
-            cost_estimate=pl.CostEstimate(flops=3 * term_flops, bytes_accessed=9 * width * width * 2, transcendentals=0),
+            cost_estimate=cost,
             name="right_mix",
-        )(own_meta, sib_meta, where_dst, mixed, right, right_sib)
+        )(meta, sib_meta, where_dst, mixed, right, right_sib)
         for j in range(1, bands):
-            keep = keep + shift(send[j - 1], band_step=j).astype(F32)
-        if d:
-            keep = keep.astype(BF16)
-            totals.append((shift(keep[0], planes=d), shift(keep[1], planes=d, flip=True)))
-        else:
-            totals.append((keep[0], shift(keep[1].astype(BF16), flip=True)))
-    same = sum(t[0].astype(F32) for t in totals)
-    cross = sum(t[1].astype(F32) for t in totals)
+            keep = keep + move(send[j - 1], band_step=j).astype(F32)
+        return keep
+
+    beside_far = right_mix(0, own_meta).astype(BF16)
+    mirrored = right_mix(1, own_meta)
+    meta, beside_far = lax.optimization_barrier((own_meta, beside_far))
+    mirrored = (mirrored + move(beside_far, beside).astype(F32)).astype(BF16)
+    beside_near = right_mix(2, meta).astype(BF16)
+    total = right_mix(3, meta) + move(mirrored, mirror).astype(F32) + move(beside_near, beside).astype(F32)
+    same, cross = total[0], move(total[1], flip=True)
     first = core == 0
     return jnp.concatenate([jnp.where(first, same, cross), jnp.where(first, cross, same)], axis=1)
 

time: 108 us -> 94.8 us (0.88)
  the two profiles are of different devices: /device:TPU:13 before, /device:TPU:0 now
where the time goes in v2:
time: 94.8 us; the launch traced here: 95.3 us
  waiting for transfers between devices  34 us (36%)
  starting transfers between devices  30.3 us (32%)
  Pallas kernels  24.4 us (26%)
  local copies, waits for them, and re-layouts  3.67 us (4%)
  other arithmetic  2.02 us (2%)
    ppermute x19, waiting for transfers between devices, move(): return lax.ppermute(value, 'term', pairs)  34 us
    ppermute x19, starting transfers between devices, move(): return lax.ppermute(value, 'term', pairs)  30.3 us
    pallas_call x4, Pallas kernels, right_mix(): pl.pallas_call(functools.partial(right_kernel, phase), out_shape=(jax.Sha...  12.7 us
    pallas_call x4, Pallas kernels, local(): pl.pallas_call(functools.partial(left_kernel, phase), out_shape=jax.Shape...  11.8 us
    unnamed x6, local copies, waits for them, and re-layouts  2.5 us
  transfers between devices with their start and end apart: 19, of which 13 were waited for; matrix products, arithmetic and copies ran while one was open for 1% of the time, Pallas kernels for 25%

profile of v2, /device:TPU:0, one launch (start us, length us, event | category | flops | bytes accessed | tf_op | source)
XLA Modules:
  0.0 95.3 jit_solution(8337522996380003639)
XLA Ops:
  0.0 1.0 %dynamic-slice_bitcast_fusion = (bf16[1,128,512]{2,1,0:T(8,128)(2,1)S(1)}, bf16[128,512]{1,0:T(8,128)(2,1)S(1)}) fusion(bf16[128,1024]{1,0:T(8,128)(2,1)} %param.6, s32[]{:T(128)S(6)} %select_n.41, s32[]{:T(128)S(6)} %select_n.42), kind=kLoop, calls=%fused_computation.10 | loop fusion | bytes 524296 | tf_op jit(solution)/shard_map/stack | solution.py:163
  1.0 0.5 collective-permute-start.1
  1.5 1.0 %collective-permute-done.1 = bf16[128,512]{1,0:T(8,128)(2,1)S(1)} collective-permute-done((bf16[128,512]{1,0:T(8,128)(2,1)S(1)}, bf16[128,512]{1,0:T(8,128)(2,1)S(1)}, u32[]{:S(2)}, u32[]{:S(2)}) %collective-permute-start.1) | collective-permute-done | bytes 131104 | tf_op jit(solution)/shard_map/ppermute | solution.py:145
  2.5 0.4 collective-permute-start.4
  2.9 4.8 %collective-permute-start.2 = (bf16[2,128,512]{2,1,0:T(8,128)(2,1)S(1)}, bf16[2,128,512]{2,1,0:T(8,128)(2,1)S(1)}, u32[]{:S(2)}, u32[]{:S(2)}) collective-permute-start(bf16[2,128,512]{2,1,0:T(8,128)(2,1)S(1)} %pad_maximum_fusion.1.refs_3_), channel_id=1, source_target_pairs={{0,12},{1,13},{2,14},{3,15},{4,8},{5,9},{6,10},{7,11},{8,4},{9,5},... | collective-permute-start | bytes 786440 | tf_op jit(solution)/shard_map/ppermute | solution.py:145
  7.7 6.9 %collective-permute-done.2.refs_3_ = bf16[2,128,512]{2,1,0:T(8,128)(2,1)S(1)} collective-permute-done((bf16[2,128,512]{2,1,0:T(8,128)(2,1)S(1)}, bf16[2,128,512]{2,1,0:T(8,128)(2,1)S(1)}, u32[]{:S(2)}, u32[]{:S(2)}) %collective-permute-start.2) | collective-permute-done | bytes 262176 | tf_op jit(solution)/shard_map/ppermute | solution.py:145
  14.6 0.0 collective-permute-start.10
  14.6 5.2 %collective-permute-start.6 = (bf16[2,128,512]{2,1,0:T(8,128)(2,1)S(1)}, bf16[2,128,512]{2,1,0:T(8,128)(2,1)S(1)}, u32[]{:S(2)}, u32[]{:S(2)}) collective-permute-start(bf16[2,128,512]{2,1,0:T(8,128)(2,1)S(1)} %pad_maximum_fusion.1.refs_3_), channel_id=1, source_target_pairs={{0,4},{1,5},{2,6},{3,7},{4,0},{5,1},{6,2},{7,3},{8,12},{9,13},{10,... | collective-permute-start | bytes 786440 | tf_op jit(solution)/shard_map/ppermute | solution.py:145
  19.9 1.5 %collective-permute-start.3 = (bf16[2,128,512]{2,1,0:T(8,128)(2,1)S(1)}, bf16[2,128,512]{2,1,0:T(8,128)(2,1)S(1)}, u32[]{:S(2)}, u32[]{:S(2)}) collective-permute-start(bf16[2,128,512]{2,1,0:T(8,128)(2,1)S(1)} %pad_maximum_fusion.1.refs_3_), channel_id=1, source_target_pairs={{0,2},{1,3},{2,0},{3,1},{4,6},{5,7},{6,4},{7,5},{8,10},{9,11},{10,... | collective-permute-start | bytes 786440 | tf_op jit(solution)/shard_map/ppermute | solution.py:145
  22.0 0.7 pad_add_fusion.refs_0_
  22.8 0.0 collective-permute-start
  22.8 0.1 stack.58.refs_2_
  22.9 0.1 stack.57.refs_2_
  23.0 0.9 collective-permute-done.refs_1_
  23.9 0.9 collective-permute-start.9
  24.7 2.1 %collective-permute-done.6.refs_3_ = bf16[2,128,512]{2,1,0:T(8,128)(2,1)S(1)} collective-permute-done((bf16[2,128,512]{2,1,0:T(8,128)(2,1)S(1)}, bf16[2,128,512]{2,1,0:T(8,128)(2,1)S(1)}, u32[]{:S(2)}, u32[]{:S(2)}) %collective-permute-start.6) | collective-permute-done | bytes 262176 | tf_op jit(solution)/shard_map/ppermute | solution.py:145
  26.8 1.5 %collective-permute-start.7 = (bf16[2,128,512]{2,1,0:T(8,128)(2,1)S(1)}, bf16[2,128,512]{2,1,0:T(8,128)(2,1)S(1)}, u32[]{:S(2)}, u32[]{:S(2)}) collective-permute-start(bf16[2,128,512]{2,1,0:T(8,128)(2,1)S(1)} %collective-permute-done.6.refs_3_), channel_id=1, source_target_pairs={{0,2},{1,3},{2,0},{3,1},{4,6},{5,7},{6,4},{7,5},{8,10},{9,11},{10,... | collective-permute-start | bytes 786440 | tf_op jit(solution)/shard_map/ppermute | solution.py:145
  28.3 0.7 collective-permute-done.3
  29.0 0.0 collective-permute-done.4.refs_6_
  29.0 0.0 copy-start
  29.0 2.5 %copy-done = bf16[10,512,512]{2,1,0:T(8,128)(2,1)S(1)} copy-done((bf16[10,512,512]{2,1,0:T(8,128)(2,1)S(1)}, bf16[10,512,512]{2,1,0:T(8,128)(2,1)}, u32[]{:S(2)}) %copy-start) | copy-done | bytes 5242904
  31.5 3.3 %left_mix.4.refs_7_ = bf16[20,512,512]{2,1,0:T(8,128)(2,1)S(1)} custom-call(s32[21]{0:T(128)S(1)} %pad_add_fusion.refs_0_, s32[21]{0:T(128)S(1)} %collective-permute-done.refs_1_, s32[6]{0:T(128)S(1)} %stack.58.refs_2_, bf16[2,128,512]{2,1,0:T(8,128)(2,1)S(1)} %pad_maximum_fusion.1.refs_3_, bf16[1,2,128,512]{3,2,1,0:T(8,128)(2,1)S(1)} %bitcast.27, ...), custom_call_target="tpu_custom_call" | custom-call | flops 4000000000 | bytes 3670016 | tf_op jit(solution)/shard_map/left_mix/pallas_call | solution.py:186
  34.8 2.5 %collective-permute-start.5 = (bf16[2,128,512]{2,1,0:T(8,128)(2,1)S(1)}, bf16[2,128,512]{2,1,0:T(8,128)(2,1)S(1)}, u32[]{:S(2)}, u32[]{:S(2)}) collective-permute-start(bf16[2,128,512]{2,1,0:T(8,128)(2,1)S(1)} %collective-permute-done.2.refs_3_), channel_id=1, source_target_pairs={{0,4},{1,5},{2,6},{3,7},{4,0},{5,1},{6,2},{7,3},{8,12},{9,13},{10,... | collective-permute-start | bytes 786440 | tf_op jit(solution)/shard_map/ppermute | solution.py:145
  37.3 2.2 %collective-permute-done.7 = bf16[2,128,512]{2,1,0:T(8,128)(2,1)S(1)} collective-permute-done((bf16[2,128,512]{2,1,0:T(8,128)(2,1)S(1)}, bf16[2,128,512]{2,1,0:T(8,128)(2,1)S(1)}, u32[]{:S(2)}, u32[]{:S(2)}) %collective-permute-start.7) | collective-permute-done | bytes 262176 | tf_op jit(solution)/shard_map/ppermute | solution.py:145
  39.5 5.8 %left_mix.5.refs_7_ = bf16[20,512,512]{2,1,0:T(8,128)(2,1)S(1)} custom-call(s32[21]{0:T(128)S(1)} %pad_add_fusion.refs_0_, s32[21]{0:T(128)S(1)} %collective-permute-done.refs_1_, s32[6]{0:T(128)S(1)} %stack.58.refs_2_, bf16[2,128,512]{2,1,0:T(8,128)(2,1)S(1)} %collective-permute-done.6.refs_3_, ...), custom_call_target="tpu_custom_call", output_to_operand_aliasing={{}: (7, {})} | custom-call | flops 4000000000 | bytes 3670016 | tf_op jit(solution)/shard_map/left_mix/pallas_call | solution.py:186
  45.4 0.0 collective-permute-done.5.refs_3_
  45.4 0.1 collective-permute-start.8
  45.5 0.0 collective-permute-done.9
  45.5 0.0 slice-start
  45.5 1.9 %left_mix.6.refs_7_ = bf16[20,512,512]{2,1,0:T(8,128)(2,1)S(1)} custom-call(s32[21]{0:T(128)S(1)} %pad_add_fusion.refs_0_, s32[21]{0:T(128)S(1)} %collective-permute-done.refs_1_, s32[6]{0:T(128)S(1)} %stack.58.refs_2_, bf16[2,128,512]{2,1,0:T(8,128)(2,1)S(1)} %collective-permute-done.2.refs_3_, ...), custom_call_target="tpu_custom_call", output_to_operand_aliasing={{}: (7, {})} | custom-call | flops 4000000000 | bytes 3670016 | tf_op jit(solution)/shard_map/left_mix/pallas_call | solution.py:186
  47.4 0.0 slice-start.1
  47.4 4.8 %collective-permute-done.8 = bf16[2,128,512]{2,1,0:T(8,128)(2,1)S(1)} collective-permute-done((bf16[2,128,512]{2,1,0:T(8,128)(2,1)S(1)}, bf16[2,128,512]{2,1,0:T(8,128)(2,1)S(1)}, u32[]{:S(2)}, u32[]{:S(2)}) %collective-permute-start.8) | collective-permute-done | bytes 262176 | tf_op jit(solution)/shard_map/ppermute | solution.py:145
  52.1 0.8 left_mix.7.refs_3_
  52.9 0.0 collective-permute-done.10.refs_5_
  52.9 0.0 slice-done
  52.9 0.0 slice-done.1
  53.0 0.9 right_mix.4
  53.9 0.9 collective-permute-start.11
  54.8 3.1 %right_mix.6 = (f32[2,128,512]{2,1,0:T(8,128)S(1)}, bf16[1,2,128,512]{3,2,1,0:T(8,128)(2,1)S(1)}) custom-call(s32[21]{0:T(128)S(1)} %pad_add_fusion.refs_0_, s32[21]{0:T(128)S(1)} %collective-permute-done.refs_1_, s32[6]{0:T(128)S(1)} %stack.57.refs_2_, bf16[20,512,512]{2,1,0:T(8,128)(2,1)S(1)} %left_mix.7.refs_3_, bf16[10,512,512]{2,1,0:T(8,128)(2,1)S(1)} %bitcast.26, ...), custom_call_target="tpu_custom_call" | custom-call | flops 4000000000 | bytes 3670016 | tf_op jit(solution)/shard_map/right_mix/pallas_call | solution.py:206
  57.9 0.5 collective-permute-start.13
  58.4 2.6 %collective-permute-done.11 = bf16[2,128,512]{2,1,0:T(8,128)(2,1)S(1)} collective-permute-done((bf16[2,128,512]{2,1,0:T(8,128)(2,1)S(1)}, bf16[2,128,512]{2,1,0:T(8,128)(2,1)S(1)}, u32[]{:S(2)}, u32[]{:S(2)}) %collective-permute-start.11) | collective-permute-done | bytes 262176 | tf_op jit(solution)/shard_map/ppermute | solution.py:145
  61.0 0.1 add_convert_fusion.2
  61.1 9.5 %collective-permute-start.14 = (bf16[2,128,512]{2,1,0:T(8,128)(2,1)S(1)}, bf16[2,128,512]{2,1,0:T(8,128)(2,1)S(1)}, u32[]{:S(2)}, u32[]{:S(2)}) collective-permute-start(bf16[2,128,512]{2,1,0:T(8,128)(2,1)S(1)} %add_convert_fusion.2), channel_id=1, source_target_pairs={{0,4},{1,5},{2,6},{3,7},{4,0},{5,1},{6,2},{7,3},{8,12},{9,13},{10,... | collective-permute-start | bytes 786440 | tf_op jit(solution)/shard_map/ppermute | solution.py:145
  70.5 4.9 %right_mix.7 = (f32[2,128,512]{2,1,0:T(8,128)S(1)}, bf16[1,2,128,512]{3,2,1,0:T(8,128)(2,1)S(1)}) custom-call(s32[21]{0:T(128)S(1)} %pad_add_fusion.refs_0_, s32[21]{0:T(128)S(1)} %collective-permute-done.refs_1_, s32[6]{0:T(128)S(1)} %stack.57.refs_2_, bf16[20,512,512]{2,1,0:T(8,128)(2,1)S(1)} %left_mix.7.refs_3_, bf16[10,512,512]{2,1,0:T(8,128)(2,1)S(1)} %bitcast.26, ...), custom_call_target="tpu_custom_call" | custom-call | flops 4000000000 | bytes 3670016 | tf_op jit(solution)/shard_map/right_mix/pallas_call | solution.py:206
  75.4 0.1 collective-permute-start.16
  75.5 3.8 %right_mix.5 = (f32[2,128,512]{2,1,0:T(8,128)S(1)}, bf16[1,2,128,512]{3,2,1,0:T(8,128)(2,1)S(1)}) custom-call(s32[21]{0:T(128)S(1)} %pad_add_fusion.refs_0_, s32[21]{0:T(128)S(1)} %collective-permute-done.refs_1_, s32[6]{0:T(128)S(1)} %stack.57.refs_2_, bf16[20,512,512]{2,1,0:T(8,128)(2,1)S(1)} %left_mix.7.refs_3_, bf16[10,512,512]{2,1,0:T(8,128)(2,1)S(1)} %bitcast.26, ...), custom_call_target="tpu_custom_call" | custom-call | flops 4000000000 | bytes 3670016 | tf_op jit(solution)/shard_map/right_mix/pallas_call | solution.py:206
  79.3 1.7 %collective-permute-start.12 = (bf16[2,128,512]{2,1,0:T(8,128)(2,1)S(1)}, bf16[2,128,512]{2,1,0:T(8,128)(2,1)S(1)}, u32[]{:S(2)}, u32[]{:S(2)}) collective-permute-start(bf16[2,128,512]{2,1,0:T(8,128)(2,1)S(1)} %bitcast.31), channel_id=1, source_target_pairs={{0,2},{1,3},{2,0},{3,1},{4,6},{5,7},{6,4},{7,5},{8,10},{9,11},{10,... | collective-permute-start | bytes 786440 | tf_op jit(solution)/shard_map/ppermute | solution.py:145
  81.0 0.0 collective-permute-done.13
  81.0 0.0 collective-permute-done.14
  81.0 0.1 add_convert_fusion.1
  81.1 0.1 collective-permute-start.15
  81.2 2.5 %collective-permute-done.16 = bf16[2,128,512]{2,1,0:T(8,128)(2,1)S(1)} collective-permute-done((bf16[2,128,512]{2,1,0:T(8,128)(2,1)S(1)}, bf16[2,128,512]{2,1,0:T(8,128)(2,1)S(1)}, u32[]{:S(2)}, u32[]{:S(2)}) %collective-permute-start.16) | collective-permute-done | bytes 262176 | tf_op jit(solution)/shard_map/ppermute | solution.py:145
  83.7 0.1 add_convert_fusion
  83.8 0.1 collective-permute-start.17
  83.9 2.7 %collective-permute-done.12 = bf16[2,128,512]{2,1,0:T(8,128)(2,1)S(1)} collective-permute-done((bf16[2,128,512]{2,1,0:T(8,128)(2,1)S(1)}, bf16[2,128,512]{2,1,0:T(8,128)(2,1)S(1)}, u32[]{:S(2)}, u32[]{:S(2)}) %collective-permute-start.12) | collective-permute-done | bytes 262176 | tf_op jit(solution)/shard_map/ppermute | solution.py:145
  86.5 3.6 %collective-permute-done.15 = bf16[2,128,512]{2,1,0:T(8,128)(2,1)S(1)} collective-permute-done((bf16[2,128,512]{2,1,0:T(8,128)(2,1)S(1)}, bf16[2,128,512]{2,1,0:T(8,128)(2,1)S(1)}, u32[]{:S(2)}, u32[]{:S(2)}) %collective-permute-start.15) | collective-permute-done | bytes 262176 | tf_op jit(solution)/shard_map/ppermute | solution.py:145
  90.1 2.5 %collective-permute-done.17 = bf16[2,128,512]{2,1,0:T(8,128)(2,1)S(1)} collective-permute-done((bf16[2,128,512]{2,1,0:T(8,128)(2,1)S(1)}, bf16[2,128,512]{2,1,0:T(8,128)(2,1)S(1)}, u32[]{:S(2)}, u32[]{:S(2)}) %collective-permute-start.17) | collective-permute-done | bytes 262176 | tf_op jit(solution)/shard_map/ppermute | solution.py:145
  92.6 0.1 convert_add_fusion
  92.8 0.1 collective-permute-start.18
  92.9 1.5 %collective-permute-done.18 = f32[128,512]{1,0:T(8,128)S(1)} collective-permute-done((f32[128,512]{1,0:T(8,128)S(1)}, f32[128,512]{1,0:T(8,128)S(1)}, u32[]{:S(2)}, u32[]{:S(2)}) %collective-permute-start.18) | collective-permute-done | bytes 262176 | tf_op jit(solution)/shard_map/ppermute | solution.py:145
  94.4 0.8 pad_maximum_fusion
  (4 shorter events, 0.1 us)
Async XLA Ops:
  1.0 1.5 %collective-permute-start.1 = (bf16[128,512]{1,0:T(8,128)(2,1)S(1)}, bf16[128,512]{1,0:T(8,128)(2,1)S(1)}, u32[]{:S(2)}, u32[]{:S(2)}) collective-permute-start(bf16[128,512]{1,0:T(8,128)(2,1)S(1)} %get-tuple-element.44), channel_id=1, source_target_pairs={{0,1},{1,0},{2,3},{3,2},{4,5},{5,4},{6,7},{7,6},{8,9},{9,8},{10,11... | collective-permute-start | bytes 393224 | tf_op jit(solution)/shard_map/ppermute | solution.py:145
  2.5 26.5 %collective-permute-start.4 = (bf16[10,512,512]{2,1,0:T(8,128)(2,1)}, bf16[10,512,512]{2,1,0:T(8,128)(2,1)}, u32[]{:S(2)}, u32[]{:S(2)}) collective-permute-start(bf16[10,512,512]{2,1,0:T(8,128)(2,1)} %refs_5_.7), channel_id=1, source_target_pairs={{0,1},{1,0},{2,3},{3,2},{4,5},{5,4},{6,7},{7,6},{8,9},{9,8},{10,11... | collective-permute-start | bytes 15728648 | tf_op jit(solution)/shard_map/ppermute | solution.py:145
  2.9 11.7 %collective-permute-start.2 = (bf16[2,128,512]{2,1,0:T(8,128)(2,1)S(1)}, bf16[2,128,512]{2,1,0:T(8,128)(2,1)S(1)}, u32[]{:S(2)}, u32[]{:S(2)}) collective-permute-start(bf16[2,128,512]{2,1,0:T(8,128)(2,1)S(1)} %pad_maximum_fusion.1.refs_3_), channel_id=1, source_target_pairs={{0,12},{1,13},{2,14},{3,15},{4,8},{5,9},{6,10},{7,11},{8,4},{9,5},... | collective-permute-start | bytes 786440 | tf_op jit(solution)/shard_map/ppermute | solution.py:145
  14.6 38.3 %collective-permute-start.10 = (bf16[10,512,512]{2,1,0:T(8,128)(2,1)}, bf16[10,512,512]{2,1,0:T(8,128)(2,1)}, u32[]{:S(2)}, u32[]{:S(2)}) collective-permute-start(bf16[10,512,512]{2,1,0:T(8,128)(2,1)} %refs_4_.7), channel_id=1, source_target_pairs={{0,1},{1,0},{2,3},{3,2},{4,5},{5,4},{6,7},{7,6},{8,9},{9,8},{10,11... | collective-permute-start | bytes 15728648 | tf_op jit(solution)/shard_map/ppermute | solution.py:145
  14.6 12.2 %collective-permute-start.6 = (bf16[2,128,512]{2,1,0:T(8,128)(2,1)S(1)}, bf16[2,128,512]{2,1,0:T(8,128)(2,1)S(1)}, u32[]{:S(2)}, u32[]{:S(2)}) collective-permute-start(bf16[2,128,512]{2,1,0:T(8,128)(2,1)S(1)} %pad_maximum_fusion.1.refs_3_), channel_id=1, source_target_pairs={{0,4},{1,5},{2,6},{3,7},{4,0},{5,1},{6,2},{7,3},{8,12},{9,13},{10,... | collective-permute-start | bytes 786440 | tf_op jit(solution)/shard_map/ppermute | solution.py:145
  19.9 9.1 %collective-permute-start.3 = (bf16[2,128,512]{2,1,0:T(8,128)(2,1)S(1)}, bf16[2,128,512]{2,1,0:T(8,128)(2,1)S(1)}, u32[]{:S(2)}, u32[]{:S(2)}) collective-permute-start(bf16[2,128,512]{2,1,0:T(8,128)(2,1)S(1)} %pad_maximum_fusion.1.refs_3_), channel_id=1, source_target_pairs={{0,2},{1,3},{2,0},{3,1},{4,6},{5,7},{6,4},{7,5},{8,10},{9,11},{10,... | collective-permute-start | bytes 786440 | tf_op jit(solution)/shard_map/ppermute | solution.py:145
  22.8 1.1 %collective-permute-start = (s32[21]{0:T(128)S(1)}, s32[21]{0:T(128)S(1)}, u32[]{:S(2)}, u32[]{:S(2)}) collective-permute-start(s32[21]{0:T(128)S(1)} %pad_add_fusion.refs_0_), channel_id=1, source_target_pairs={{0,1},{1,0},{2,3},{3,2},{4,5},{5,4},{6,7},{7,6},{8,9},{9,8},{10,11... | collective-permute-start | bytes 260 | tf_op jit(solution)/shard_map/ppermute | solution.py:145
  23.9 21.6 %collective-permute-start.9 = (bf16[2,128,512]{2,1,0:T(8,128)(2,1)S(1)}, bf16[2,128,512]{2,1,0:T(8,128)(2,1)S(1)}, u32[]{:S(2)}, u32[]{:S(2)}) collective-permute-start(bf16[2,128,512]{2,1,0:T(8,128)(2,1)S(1)} %collective-permute-done.2.refs_3_), channel_id=1, source_target_pairs={{0,2},{1,3},{2,0},{3,1},{4,6},{5,7},{6,4},{7,5},{8,10},{9,11},{10,... | collective-permute-start | bytes 786440 | tf_op jit(solution)/shard_map/ppermute | solution.py:145
  26.8 12.7 %collective-permute-start.7 = (bf16[2,128,512]{2,1,0:T(8,128)(2,1)S(1)}, bf16[2,128,512]{2,1,0:T(8,128)(2,1)S(1)}, u32[]{:S(2)}, u32[]{:S(2)}) collective-permute-start(bf16[2,128,512]{2,1,0:T(8,128)(2,1)S(1)} %collective-permute-done.6.refs_3_), channel_id=1, source_target_pairs={{0,2},{1,3},{2,0},{3,1},{4,6},{5,7},{6,4},{7,5},{8,10},{9,11},{10,... | collective-permute-start | bytes 786440 | tf_op jit(solution)/shard_map/ppermute | solution.py:145
  29.0 2.5 %copy-start = (bf16[10,512,512]{2,1,0:T(8,128)(2,1)S(1)}, bf16[10,512,512]{2,1,0:T(8,128)(2,1)}, u32[]{:S(2)}) copy-start(bf16[10,512,512]{2,1,0:T(8,128)(2,1)} %refs_5_.7) | copy-start | bytes 15728644
  34.8 10.6 %collective-permute-start.5 = (bf16[2,128,512]{2,1,0:T(8,128)(2,1)S(1)}, bf16[2,128,512]{2,1,0:T(8,128)(2,1)S(1)}, u32[]{:S(2)}, u32[]{:S(2)}) collective-permute-start(bf16[2,128,512]{2,1,0:T(8,128)(2,1)S(1)} %collective-permute-done.2.refs_3_), channel_id=1, source_target_pairs={{0,4},{1,5},{2,6},{3,7},{4,0},{5,1},{6,2},{7,3},{8,12},{9,13},{10,... | collective-permute-start | bytes 786440 | tf_op jit(solution)/shard_map/ppermute | solution.py:145
  45.4 6.7 %collective-permute-start.8 = (bf16[2,128,512]{2,1,0:T(8,128)(2,1)S(1)}, bf16[2,128,512]{2,1,0:T(8,128)(2,1)S(1)}, u32[]{:S(2)}, u32[]{:S(2)}) collective-permute-start(bf16[2,128,512]{2,1,0:T(8,128)(2,1)S(1)} %collective-permute-done.5.refs_3_), channel_id=1, source_target_pairs={{0,2},{1,3},{2,0},{3,1},{4,6},{5,7},{6,4},{7,5},{8,10},{9,11},{10,... | collective-permute-start | bytes 786440 | tf_op jit(solution)/shard_map/ppermute | solution.py:145
  45.5 7.4 %slice-start = ((s8[5242880]{0:T(1024)(128)(4,1)}), s8[4194304]{0:T(1024)(128)(4,1)S(1)}, s32[]{:S(2)}) async-start(s8[5242880]{0:T(1024)(128)(4,1)} %bitcast.25), calls=%async_computation | async-start | bytes 8388608
  47.4 5.6 %slice-start.1 = ((s8[5242880]{0:T(1024)(128)(4,1)}), s8[1048576]{0:T(1024)(128)(4,1)S(1)}, s32[]{:S(2)}) async-start(s8[5242880]{0:T(1024)(128)(4,1)} %bitcast.25), calls=%async_computation.1 | async-start | bytes 2097152
  53.9 7.1 %collective-permute-start.11 = (bf16[2,128,512]{2,1,0:T(8,128)(2,1)S(1)}, bf16[2,128,512]{2,1,0:T(8,128)(2,1)S(1)}, u32[]{:S(2)}, u32[]{:S(2)}) collective-permute-start(bf16[2,128,512]{2,1,0:T(8,128)(2,1)S(1)} %bitcast.34), channel_id=1, source_target_pairs={{0,2},{1,3},{2,0},{3,1},{4,6},{5,7},{6,4},{7,5},{8,10},{9,11},{10,... | collective-permute-start | bytes 786440 | tf_op jit(solution)/shard_map/ppermute | solution.py:145
  57.9 23.1 %collective-permute-start.13 = (bf16[2,128,512]{2,1,0:T(8,128)(2,1)S(1)}, bf16[2,128,512]{2,1,0:T(8,128)(2,1)S(1)}, u32[]{:S(2)}, u32[]{:S(2)}) collective-permute-start(bf16[2,128,512]{2,1,0:T(8,128)(2,1)S(1)} %bitcast.32), channel_id=1, source_target_pairs={{0,2},{1,3},{2,0},{3,1},{4,6},{5,7},{6,4},{7,5},{8,10},{9,11},{10,... | collective-permute-start | bytes 786440 | tf_op jit(solution)/shard_map/ppermute | solution.py:145
  61.1 19.9 %collective-permute-start.14 = (bf16[2,128,512]{2,1,0:T(8,128)(2,1)S(1)}, bf16[2,128,512]{2,1,0:T(8,128)(2,1)S(1)}, u32[]{:S(2)}, u32[]{:S(2)}) collective-permute-start(bf16[2,128,512]{2,1,0:T(8,128)(2,1)S(1)} %add_convert_fusion.2), channel_id=1, source_target_pairs={{0,4},{1,5},{2,6},{3,7},{4,0},{5,1},{6,2},{7,3},{8,12},{9,13},{10,... | collective-permute-start | bytes 786440 | tf_op jit(solution)/shard_map/ppermute | solution.py:145
  75.4 8.3 %collective-permute-start.16 = (bf16[2,128,512]{2,1,0:T(8,128)(2,1)S(1)}, bf16[2,128,512]{2,1,0:T(8,128)(2,1)S(1)}, u32[]{:S(2)}, u32[]{:S(2)}) collective-permute-start(bf16[2,128,512]{2,1,0:T(8,128)(2,1)S(1)} %bitcast.33), channel_id=1, source_target_pairs={{0,2},{1,3},{2,0},{3,1},{4,6},{5,7},{6,4},{7,5},{8,10},{9,11},{10,... | collective-permute-start | bytes 786440 | tf_op jit(solution)/shard_map/ppermute | solution.py:145
  79.3 7.2 %collective-permute-start.12 = (bf16[2,128,512]{2,1,0:T(8,128)(2,1)S(1)}, bf16[2,128,512]{2,1,0:T(8,128)(2,1)S(1)}, u32[]{:S(2)}, u32[]{:S(2)}) collective-permute-start(bf16[2,128,512]{2,1,0:T(8,128)(2,1)S(1)} %bitcast.31), channel_id=1, source_target_pairs={{0,2},{1,3},{2,0},{3,1},{4,6},{5,7},{6,4},{7,5},{8,10},{9,11},{10,... | collective-permute-start | bytes 786440 | tf_op jit(solution)/shard_map/ppermute | solution.py:145
  81.1 9.0 %collective-permute-start.15 = (bf16[2,128,512]{2,1,0:T(8,128)(2,1)S(1)}, bf16[2,128,512]{2,1,0:T(8,128)(2,1)S(1)}, u32[]{:S(2)}, u32[]{:S(2)}) collective-permute-start(bf16[2,128,512]{2,1,0:T(8,128)(2,1)S(1)} %add_convert_fusion.1), channel_id=1, source_target_pairs={{0,12},{1,13},{2,14},{3,15},{4,8},{5,9},{6,10},{7,11},{8,4},{9,5},... | collective-permute-start | bytes 786440 | tf_op jit(solution)/shard_map/ppermute | solution.py:145
  83.8 8.8 %collective-permute-start.17 = (bf16[2,128,512]{2,1,0:T(8,128)(2,1)S(1)}, bf16[2,128,512]{2,1,0:T(8,128)(2,1)S(1)}, u32[]{:S(2)}, u32[]{:S(2)}) collective-permute-start(bf16[2,128,512]{2,1,0:T(8,128)(2,1)S(1)} %add_convert_fusion), channel_id=1, source_target_pairs={{0,4},{1,5},{2,6},{3,7},{4,0},{5,1},{6,2},{7,3},{8,12},{9,13},{10,... | collective-permute-start | bytes 786440 | tf_op jit(solution)/shard_map/ppermute | solution.py:145
  92.8 1.6 %collective-permute-start.18 = (f32[128,512]{1,0:T(8,128)S(1)}, f32[128,512]{1,0:T(8,128)S(1)}, u32[]{:S(2)}, u32[]{:S(2)}) collective-permute-start(f32[128,512]{1,0:T(8,128)S(1)} %slice_bitcast_fusion), channel_id=1, source_target_pairs={{0,1},{1,0},{2,3},{3,2},{4,5},{5,4},{6,7},{7,6},{8,9},{9,8},{10,11... | collective-permute-start | bytes 786440 | tf_op jit(solution)/shard_map/ppermute | solution.py:145

commit v3 on v2

v3 whole, which is shorter than its diff:
```python
import functools

import jax
import jax.numpy as jnp
from jax import lax
from jax.experimental import pallas as pl
from jax.experimental.pallas import tpu as pltpu
from jax.sharding import PartitionSpec as P

F32, BF16 = jnp.float32, jnp.bfloat16
CORES = 2
HALVES = 2
VMEM = 16 * 1024 * 1024
ANY = pl.BlockSpec(memory_space=pl.ANY)
SMEM = pl.BlockSpec(memory_space=pltpu.SMEM)
WHOLE = pl.BlockSpec(memory_space=pltpu.VMEM)


def list_slots(own, sib, field, sector, slots, found):
    def look(t, count):
        found[count] = t
        hit = jnp.logical_and(t < own[2 * slots], own[field * slots + t] == sector)
        count = count + hit.astype(jnp.int32)
        found[count] = t + slots
        hit = jnp.logical_and(t < sib[2 * slots], sib[field * slots + t] == sector)
        return count + hit.astype(jnp.int32)

    return lax.fori_loop(0, slots, look, jnp.int32(0))


def start_fetch(term, slots, own_hbm, sib_hbm, target, sem):
    @pl.when(term < slots)
    def _():
        pltpu.make_async_copy(own_hbm.at[term], target, sem).start()

    @pl.when(term >= slots)
    def _():
        pltpu.make_async_copy(sib_hbm.at[term - slots], target, sem).start()


def left_kernel(own, sib, source, left, left_sib, mixed, lbuf, obuf, lsem, osem):
    slots, depth, width = left.shape[0], lbuf.shape[0], left.shape[1]
    mine = own[2 * slots]
    count = mine + sib[2 * slots]

    def term(i):
        return jnp.where(i < mine, i, i - mine + slots)

    for i in range(depth - 1):
        @pl.when(i < count)
        def _():
            start_fetch(term(i), slots, left, left_sib, lbuf.at[i], lsem.at[i])

    def out_copy(i):
        return pltpu.make_async_copy(obuf.at[lax.rem(i, 2)], mixed.at[term(i)], osem.at[lax.rem(i, 2)])

    def step(i, carry):
        ahead = i + depth - 1
        @pl.when(ahead < count)
        def _():
            k = lax.rem(ahead, depth)
            start_fetch(term(ahead), slots, left, left_sib, lbuf.at[k], lsem.at[k])

        k = lax.rem(i, depth)
        pltpu.make_async_copy(left.at[0], lbuf.at[k], lsem.at[k]).wait()

        @pl.when(i >= 2)
        def _():
            out_copy(i - 2).wait()

        sector = jnp.where(i < mine, own[jnp.minimum(i, slots - 1)], sib[jnp.clip(i - mine, 0, slots - 1)])
        block = source[pl.ds(pl.multiple_of(sector * width, width), width)]
        obuf[lax.rem(i, 2)] = jnp.dot(lbuf[k], block, preferred_element_type=F32).astype(BF16)
        out_copy(i).start()
        return carry

    lax.fori_loop(0, count, step, 0)
    for back in (2, 1):
        @pl.when(count >= back)
        def _():
            out_copy(count - back).wait()


def right_kernel(phase, *refs):
    own, sib, where, mixed_a, mixed_b, right, right_sib, keep, send, found, acc, mbuf, rbuf, msem, rsem = refs
    slots, depth = right.shape[0], rbuf.shape[0]
    half = keep.shape[1]
    bands = send.shape[0] + 1
    sector, band, core = where[phase], where[where.shape[0] - 2], where[where.shape[0] - 1]
    count = list_slots(own, sib, 1, sector, slots, found)

    def fetch(i, k):
        term = found[i]
        for h, mixed in enumerate((mixed_a, mixed_b)):
            pltpu.make_async_copy(mixed.at[term], mbuf.at[k, h], msem.at[k, h]).start()
        start_fetch(term, slots, right, right_sib, rbuf.at[k], rsem.at[k])

    for i in range(depth - 1):
        @pl.when(i < count)
        def _():
            fetch(i, i)
    acc[...] = jnp.zeros_like(acc)

    def step(i, carry):
        ahead = i + depth - 1
        @pl.when(ahead < count)
        def _():
            fetch(ahead, lax.rem(ahead, depth))

        k = lax.rem(i, depth)
        for h, mixed in enumerate((mixed_a, mixed_b)):
            pltpu.make_async_copy(mixed.at[0], mbuf.at[k, h], msem.at[k, h]).wait()
        pltpu.make_async_copy(right.at[0], rbuf.at[k], rsem.at[k]).wait()
        part = mbuf.shape[3]
        acc[...] += sum(
            lax.dot_general(
                mbuf[k, h], rbuf[k, :, h * part : (h + 1) * part], (((1,), (1,)), ((), ())), preferred_element_type=F32
            )
            for h in range(HALVES)
        )
        return carry

    lax.fori_loop(0, count, step, 0)
    for j in range(bands):
        b = lax.rem(band + j, bands)
        for i in range(CORES):
            c = core if i == 0 else 1 - core
            rows = acc[pl.ds(pl.multiple_of((b * CORES + c) * half, half), half)]
            if j == 0:
                keep[i] = rows
            else:
                send[j - 1, i] = rows.astype(BF16)


def local(devices, wavefunction, left, right, src, dst, live):
    slots, width = left.shape[0], left.shape[1]
    half = wavefunction.shape[0]
    sectors = half * devices // width
    bands = devices // (sectors * CORES)
    assert sectors == 4
    me = lax.axis_index("term")
    core, band, plane = me % CORES, (me // CORES) % bands, me // (CORES * bands)

    def move(value, to_plane=lambda a: a, band_step=0, flip=False):
        pairs = []
        for i in range(devices):
            c, b, a = i % CORES, (i // CORES) % bands, i // (CORES * bands)
            c = 1 - c if flip else c
            pairs.append((i, (to_plane(a) * bands + (b + band_step) % bands) * CORES + c))
        return lax.ppermute(value, "term", pairs)

    def beside(a):
        return a ^ 1

    def mirror(a):
        return 3 - a

    own_meta = jnp.concatenate([src, dst, live])
    sib_meta = move(own_meta, flip=True)
    mine = lax.dynamic_slice_in_dim(wavefunction, core * width, width, 1)
    theirs = lax.dynamic_slice_in_dim(wavefunction, (1 - core) * width, width, 1)
    from_sib = move(theirs, flip=True)
    left_sib, right_sib, from_sib = lax.optimization_barrier((left, right, from_sib))
    left_sib, right_sib = move(left_sib, flip=True), move(right_sib, flip=True)
    pair = jnp.stack([jnp.where(core == 0, mine, from_sib), jnp.where(core == 0, from_sib, mine)])
    part = width // HALVES
    groups = [[c + CORES * chip for chip in range(devices // CORES)] for c in range(CORES)]
    sources = [
        lax.all_gather(
            pair[:, :, h * part : (h + 1) * part].reshape(CORES * half, part),
            "term", axis=0, tiled=True, axis_index_groups=groups,
        )
        for h in range(HALVES)
    ]
    partner = plane ^ 1
    where_dst = jnp.stack([3 - partner, 3 - plane, partner, plane, band, core]).astype(jnp.int32)

    params = pltpu.CompilerParams(vmem_limit_bytes=VMEM)
    cost = pl.CostEstimate(flops=4 * 10**9, bytes_accessed=7 * width * width * 2, transcendentals=0)
    depth = 4
    mixed = [
        pl.pallas_call(
            left_kernel,
            out_shape=jax.ShapeDtypeStruct((CORES * slots, width, part), BF16),
            in_specs=[SMEM] * 2 + [WHOLE] + [ANY] * 2,
            out_specs=ANY,
            scratch_shapes=[
                pltpu.VMEM((depth, width, width), BF16),
                pltpu.VMEM((2, width, part), BF16),
                pltpu.SemaphoreType.DMA((depth,)),
                pltpu.SemaphoreType.DMA((2,)),
            ],
            compiler_params=params,
            cost_estimate=cost,
            name="left_mix",
        )(own_meta, sib_meta, source, left, left_sib)
        for source in sources
    ]

    def right_mix(phase, meta):
        keep, send = pl.pallas_call(
            functools.partial(right_kernel, phase),
            out_shape=(
                jax.ShapeDtypeStruct((CORES, half, width), F32),
                jax.ShapeDtypeStruct((bands - 1, CORES, half, width), BF16),
            ),
            in_specs=[SMEM] * 3 + [ANY] * 4,
            out_specs=(WHOLE, WHOLE),
            scratch_shapes=[
                pltpu.SMEM((CORES * slots + 1,), jnp.int32),
                pltpu.VMEM((width, width), F32),
                pltpu.VMEM((depth, HALVES, width, part), BF16),
                pltpu.VMEM((depth, width, width), BF16),
                pltpu.SemaphoreType.DMA((depth, HALVES)),
                pltpu.SemaphoreType.DMA((depth,)),
            ],
            compiler_params=params,
            cost_estimate=cost,
            name="right_mix",
        )(meta, sib_meta, where_dst, *mixed, right, right_sib)
        for j in range(1, bands):
            keep = keep + move(send[j - 1], band_step=j).astype(F32)
        return keep

    beside_far = right_mix(0, own_meta).astype(BF16)
    mirrored = right_mix(1, own_meta)
    meta, beside_far = lax.optimization_barrier((own_meta, beside_far))
    mirrored = (mirrored + move(beside_far, beside).astype(F32)).astype(BF16)
    beside_near = right_mix(2, meta).astype(BF16)
    total = right_mix(3, meta) + move(mirrored, mirror).astype(F32) + move(beside_near, beside).astype(F32)
    same, cross = total[0], move(total[1], flip=True)
    first = core == 0
    return jnp.concatenate([jnp.where(first, same, cross), jnp.where(first, cross, same)], axis=1)


def solution(mesh):
    spec = P(("parts", "term"))
    return jax.shard_map(
        functools.partial(local, mesh.shape["term"]),
        mesh=mesh,
        in_specs=(spec,) * 6,
        out_specs=spec,
        check_vma=False,
    )
```

time: 94.8 us -> 155 us (1.64)
  the two profiles are of different devices: /device:TPU:0 before, /device:TPU:13 now
where the time goes in v3:
time: 155 us; the launch traced here: 152 us
  waiting for transfers between devices  76.7 us (49%)
  Pallas kernels  28.2 us (18%)
  starting transfers between devices  16.2 us (10%)
  between operations  14.2 us (9%)
  local copies, waits for them, and re-layouts  13.2 us (9%)
  other arithmetic  3.68 us (2%)
    all_gather x2, waiting for transfers between devices, local(): lax.all_gather(pair[:, :, h * part:(h + 1) * part].reshape(CORES * half,...  61.2 us
    ppermute x12, starting transfers between devices, move(): return lax.ppermute(value, 'term', pairs)  16.2 us
    ppermute x12, waiting for transfers between devices, move(): return lax.ppermute(value, 'term', pairs)  14.9 us
    pallas_call x4, Pallas kernels, right_mix(): pl.pallas_call(functools.partial(right_kernel, phase), out_shape=(jax.Sha...  14.4 us
    pallas_call x2, Pallas kernels, local(): pl.pallas_call(left_kernel, out_shape=jax.ShapeDtypeStruct((CORES * slots...  13.9 us
    unnamed x14, local copies, waits for them, and re-layouts  12.2 us
  transfers between devices with their start and end apart: 14, of which 10 were waited for; matrix products, arithmetic and copies ran while one was open for 2% of the time, Pallas kernels for 15%

profile of v3, /device:TPU:13, one launch (start us, length us, event | category | flops | bytes accessed | tf_op | source)
XLA Modules:
  0.0 152.3 jit_solution(16604077059792161456)
XLA Ops:
  6.5 0.0 all-gather.3.cloned.1.call-start
  6.5 0.9 constant_dynamic-slice_fusion
  7.5 0.7 collective-permute-start.1
  8.2 1.0 collective-permute-done.1
  9.2 0.4 collective-permute-start.2
  9.5 0.1 collective-permute-start.3
  9.7 0.9 select_bitcast_fusion
  10.6 0.7 pad_maximum_fusion.1
  11.3 0.0 all-gather.3.cloned.1.call-update
  11.4 0.0 all-gather.5.cloned.1.call-start
  11.4 0.7 all-gather.5.cloned.1.call-update
  12.8 0.7 pad_add_fusion.own.refs_0_
  13.5 0.4 collective-permute-start
  13.9 0.1 stack.36.refs_2_
  14.0 3.9 %collective-permute-done.sib.refs_1_ = s32[21]{0:T(128)S(1)} collective-permute-done((s32[21]{0:T(128)S(1)}, s32[21]{0:T(128)S(1)}, u32[]{:S(2)}, u32[]{:S(2)}) %collective-permute-start) | collective-permute-done | bytes 116 | tf_op jit(solution)/shard_map/ppermute | solution.py:150
  17.8 33.0 %all-gather.3.cloned.1.call-done.source = bf16[2048,256]{1,0:T(8,128)(2,1)} async-done(((bf16[256,256]{1,0:T(8,128)(2,1)}), bf16[2048,256]{1,0:T(8,128)(2,1)}) %all-gather.3.cloned.1.call-update) | async-done | bytes 1048592 | tf_op jit(solution)/shard_map/all_gather | solution.py:169
  50.8 0.0 collective-permute-done.2.left_sib
  50.8 0.0 copy-start.3
  50.8 2.5 %copy-done.3 = bf16[10,512,512]{2,1,0:T(8,128)(2,1)S(1)} copy-done((bf16[10,512,512]{2,1,0:T(8,128)(2,1)S(1)}, bf16[10,512,512]{2,1,0:T(8,128)(2,1)}, u32[]{:S(2)}) %copy-start.3) | copy-done | bytes 5242904
  53.3 0.0 copy-start.5
  53.3 1.2 copy-done.5
  54.6 6.9 %left_mix.2.refs_3_ = bf16[20,512,256]{2,1,0:T(8,128)(2,1)S(1)} custom-call(s32[21]{0:T(128)S(1)} %pad_add_fusion.own.refs_0_, s32[21]{0:T(128)S(1)} %collective-permute-done.sib.refs_1_, bf16[2048,256]{1,0:T(8,128)(2,1)S(1)} %copy-done.5, bf16[10,512,512]{2,1,0:T(8,128)(2,1)S(1)} %copy-done.3, bf16[10,512,512]{2,1,0:T(8,128)(2,1)} %collective-permute-done.2.left_sib), custom_call_target="tpu_custom_call" | custom-call | flops 4000000000 | bytes 3670016 | tf_op jit(solution)/shard_map/left_mix/pallas_call | solution.py:182
  61.5 0.0 copy-start
  61.5 2.3 %copy-done = bf16[20,512,256]{2,1,0:T(8,128)(2,1)} copy-done((bf16[20,512,256]{2,1,0:T(8,128)(2,1)}, bf16[20,512,256]{2,1,0:T(8,128)(2,1)S(1)}, u32[]{:S(2)}) %copy-start) | copy-done | bytes 5242904
  63.8 28.1 %all-gather.5.cloned.1.call-done.source = bf16[2048,256]{1,0:T(8,128)(2,1)} async-done(((bf16[256,256]{1,0:T(8,128)(2,1)}), bf16[2048,256]{1,0:T(8,128)(2,1)}) %all-gather.5.cloned.1.call-update) | async-done | bytes 1048592 | tf_op jit(solution)/shard_map/all_gather | solution.py:169
  92.0 0.0 copy-start.4
  92.0 2.5 %copy-done.4 = bf16[10,512,512]{2,1,0:T(8,128)(2,1)S(1)} copy-done((bf16[10,512,512]{2,1,0:T(8,128)(2,1)S(1)}, bf16[10,512,512]{2,1,0:T(8,128)(2,1)}, u32[]{:S(2)}) %copy-start.4) | copy-done | bytes 5242904
  94.5 0.0 copy-start.6
  94.5 1.2 copy-done.6
  95.7 0.0 copy-start.1
  95.7 6.9 %left_mix.3.refs_4_ = bf16[20,512,256]{2,1,0:T(8,128)(2,1)S(1)} custom-call(s32[21]{0:T(128)S(1)} %pad_add_fusion.own.refs_0_, s32[21]{0:T(128)S(1)} %collective-permute-done.sib.refs_1_, bf16[2048,256]{1,0:T(8,128)(2,1)S(1)} %copy-done.6, bf16[10,512,512]{2,1,0:T(8,128)(2,1)S(1)} %copy-done.4, bf16[10,512,512]{2,1,0:T(8,128)(2,1)} %collective-permute-done.2.left_sib), custom_call_target="tpu_custom_call" | custom-call | flops 4000000000 | bytes 3670016 | tf_op jit(solution)/shard_map/left_mix/pallas_call | solution.py:182
  102.6 0.0 collective-permute-done.3.refs_6_
  102.6 0.0 copy-done.1
  102.6 0.0 copy-start.2
  102.7 2.5 %copy-done.2 = bf16[10,512,512]{2,1,0:T(8,128)(2,1)S(1)} copy-done((bf16[10,512,512]{2,1,0:T(8,128)(2,1)S(1)}, bf16[10,512,512]{2,1,0:T(8,128)(2,1)}, u32[]{:S(2)}) %copy-start.2) | copy-done | bytes 5242904
  105.1 5.4 %right_mix.4 = (f32[2,128,512]{2,1,0:T(8,128)S(1)}, bf16[1,2,128,512]{3,2,1,0:T(8,128)(2,1)S(1)}) custom-call(s32[21]{0:T(128)S(1)} %pad_add_fusion.own.refs_0_, s32[21]{0:T(128)S(1)} %collective-permute-done.sib.refs_1_, s32[6]{0:T(128)S(1)} %stack.36.refs_2_, bf16[20,512,256]{2,1,0:T(8,128)(2,1)S(1)} %copy-done.1, ...), custom_call_target="tpu_custom_call" | custom-call | flops 4000000000 | bytes 3670016 | tf_op jit(solution)/shard_map/right_mix/pallas_call | solution.py:201
  110.6 0.1 collective-permute-start.4
  110.7 3.4 %right_mix.6 = (f32[2,128,512]{2,1,0:T(8,128)S(1)}, bf16[1,2,128,512]{3,2,1,0:T(8,128)(2,1)S(1)}) custom-call(s32[21]{0:T(128)S(1)} %pad_add_fusion.own.refs_0_, s32[21]{0:T(128)S(1)} %collective-permute-done.sib.refs_1_, s32[6]{0:T(128)S(1)} %stack.36.refs_2_, bf16[20,512,256]{2,1,0:T(8,128)(2,1)S(1)} %copy-done.1, ...), custom_call_target="tpu_custom_call" | custom-call | flops 4000000000 | bytes 3670016 | tf_op jit(solution)/shard_map/right_mix/pallas_call | solution.py:201
  114.1 1.4 collective-permute-start.6
  115.5 2.2 %collective-permute-done.4 = bf16[2,128,512]{2,1,0:T(8,128)(2,1)S(1)} collective-permute-done((bf16[2,128,512]{2,1,0:T(8,128)(2,1)S(1)}, bf16[2,128,512]{2,1,0:T(8,128)(2,1)S(1)}, u32[]{:S(2)}, u32[]{:S(2)}) %collective-permute-start.4) | collective-permute-done | bytes 262176 | tf_op jit(solution)/shard_map/ppermute | solution.py:150
  117.7 0.1 add_convert_fusion.2
  117.8 3.4 %right_mix.7 = (f32[2,128,512]{2,1,0:T(8,128)S(1)}, bf16[1,2,128,512]{3,2,1,0:T(8,128)(2,1)S(1)}) custom-call(s32[21]{0:T(128)S(1)} %pad_add_fusion.own.refs_0_, s32[21]{0:T(128)S(1)} %collective-permute-done.sib.refs_1_, s32[6]{0:T(128)S(1)} %stack.36.refs_2_, bf16[20,512,256]{2,1,0:T(8,128)(2,1)S(1)} %copy-done.1, ...), custom_call_target="tpu_custom_call" | custom-call | flops 4000000000 | bytes 3670016 | tf_op jit(solution)/shard_map/right_mix/pallas_call | solution.py:201
  121.3 0.6 collective-permute-start.9
  121.8 0.0 collective-permute-start.7
  121.8 2.0 %right_mix.5 = (f32[2,128,512]{2,1,0:T(8,128)S(1)}, bf16[1,2,128,512]{3,2,1,0:T(8,128)(2,1)S(1)}) custom-call(s32[21]{0:T(128)S(1)} %pad_add_fusion.own.refs_0_, s32[21]{0:T(128)S(1)} %collective-permute-done.sib.refs_1_, s32[6]{0:T(128)S(1)} %stack.36.refs_2_, bf16[20,512,256]{2,1,0:T(8,128)(2,1)S(1)} %copy-done.1, ...), custom_call_target="tpu_custom_call" | custom-call | flops 4000000000 | bytes 3670016 | tf_op jit(solution)/shard_map/right_mix/pallas_call | solution.py:201
  123.9 1.9 %collective-permute-start.5 = (bf16[2,128,512]{2,1,0:T(8,128)(2,1)S(1)}, bf16[2,128,512]{2,1,0:T(8,128)(2,1)S(1)}, u32[]{:S(2)}, u32[]{:S(2)}) collective-permute-start(bf16[2,128,512]{2,1,0:T(8,128)(2,1)S(1)} %bitcast.25), channel_id=1, source_target_pairs={{0,2},{1,3},{2,0},{3,1},{4,6},{5,7},{6,4},{7,5},{8,10},{9,11},{10,... | collective-permute-start | bytes 786440 | tf_op jit(solution)/shard_map/ppermute | solution.py:150
  125.8 1.3 collective-permute-done.9
  127.1 0.1 add_convert_fusion
  127.2 0.1 collective-permute-start.10
  127.3 0.0 collective-permute-done.6
  127.3 0.0 collective-permute-done.7
  127.3 0.1 add_convert_fusion.1
  127.4 1.3 collective-permute-start.8
  128.7 3.9 %collective-permute-done.5 = bf16[2,128,512]{2,1,0:T(8,128)(2,1)S(1)} collective-permute-done((bf16[2,128,512]{2,1,0:T(8,128)(2,1)S(1)}, bf16[2,128,512]{2,1,0:T(8,128)(2,1)S(1)}, u32[]{:S(2)}, u32[]{:S(2)}) %collective-permute-start.5) | collective-permute-done | bytes 262176 | tf_op jit(solution)/shard_map/ppermute | solution.py:150
  132.6 1.1 collective-permute-done.10
  133.7 0.5 collective-permute-done.8
  134.1 0.1 convert_add_fusion
  134.3 9.2 %collective-permute-start.11 = (f32[128,512]{1,0:T(8,128)S(1)}, f32[128,512]{1,0:T(8,128)S(1)}, u32[]{:S(2)}, u32[]{:S(2)}) collective-permute-start(f32[128,512]{1,0:T(8,128)S(1)} %slice_bitcast_fusion), channel_id=1, source_target_pairs={{0,1},{1,0},{2,3},{3,2},{4,5},{5,4},{6,7},{7,6},{8,9},{9,8},{10,11... | collective-permute-start | bytes 786440 | tf_op jit(solution)/shard_map/ppermute | solution.py:150
  143.4 1.2 collective-permute-done.11
  144.7 0.8 pad_maximum_fusion
  (2 shorter events, 0.1 us)
Async XLA Ops:
  6.5 44.3 %all-gather.3.cloned.1.call-start = ((), (), s32[]{:S(2)}) async-start(), calls=%async_computation | async-start | bytes 1179648 | tf_op jit(solution)/shard_map/all_gather | solution.py:169
  7.5 1.7 %collective-permute-start.1 = (bf16[128,512]{1,0:T(8,128)(2,1)S(1)}, bf16[128,512]{1,0:T(8,128)(2,1)S(1)}, u32[]{:S(2)}, u32[]{:S(2)}) collective-permute-start(bf16[128,512]{1,0:T(8,128)(2,1)S(1)} %constant_dynamic-slice_fusion), channel_id=1, source_target_pairs={{0,1},{1,0},{2,3},{3,2},{4,5},{5,4},{6,7},{7,6},{8,9},{9,8},{10,11... | collective-permute-start | bytes 393224 | tf_op jit(solution)/shard_map/ppermute | solution.py:150
  9.2 41.7 %collective-permute-start.2 = (bf16[10,512,512]{2,1,0:T(8,128)(2,1)}, bf16[10,512,512]{2,1,0:T(8,128)(2,1)}, u32[]{:S(2)}, u32[]{:S(2)}) collective-permute-start(bf16[10,512,512]{2,1,0:T(8,128)(2,1)} %left.3), channel_id=1, source_target_pairs={{0,1},{1,0},{2,3},{3,2},{4,5},{5,4},{6,7},{7,6},{8,9},{9,8},{10,11... | collective-permute-start | bytes 15728648 | tf_op jit(solution)/shard_map/ppermute | solution.py:150
  9.5 93.1 %collective-permute-start.3 = (bf16[10,512,512]{2,1,0:T(8,128)(2,1)}, bf16[10,512,512]{2,1,0:T(8,128)(2,1)}, u32[]{:S(2)}, u32[]{:S(2)}) collective-permute-start(bf16[10,512,512]{2,1,0:T(8,128)(2,1)} %refs_5_.7), channel_id=1, source_target_pairs={{0,1},{1,0},{2,3},{3,2},{4,5},{5,4},{6,7},{7,6},{8,9},{9,8},{10,11... | collective-permute-start | bytes 15728648 | tf_op jit(solution)/shard_map/ppermute | solution.py:150
  11.4 80.6 %all-gather.5.cloned.1.call-start = ((), (), s32[]{:S(2)}) async-start(), calls=%async_computation.1 | async-start | bytes 1179648 | tf_op jit(solution)/shard_map/all_gather | solution.py:169
  13.5 4.3 %collective-permute-start = (s32[21]{0:T(128)S(1)}, s32[21]{0:T(128)S(1)}, u32[]{:S(2)}, u32[]{:S(2)}) collective-permute-start(s32[21]{0:T(128)S(1)} %pad_add_fusion.own.refs_0_), channel_id=1, source_target_pairs={{0,1},{1,0},{2,3},{3,2},{4,5},{5,4},{6,7},{7,6},{8,9},{9,8},{10,11... | collective-permute-start | bytes 260 | tf_op jit(solution)/shard_map/ppermute | solution.py:150
  50.8 2.5 %copy-start.3 = (bf16[10,512,512]{2,1,0:T(8,128)(2,1)S(1)}, bf16[10,512,512]{2,1,0:T(8,128)(2,1)}, u32[]{:S(2)}) copy-start(bf16[10,512,512]{2,1,0:T(8,128)(2,1)} %left.3) | copy-start | bytes 15728644
  53.3 1.2 copy-start.5
  61.5 2.3 %copy-start = (bf16[20,512,256]{2,1,0:T(8,128)(2,1)}, bf16[20,512,256]{2,1,0:T(8,128)(2,1)S(1)}, u32[]{:S(2)}) copy-start(bf16[20,512,256]{2,1,0:T(8,128)(2,1)S(1)} %left_mix.2.refs_3_) | copy-start | bytes 15728644
  92.0 2.5 %copy-start.4 = (bf16[10,512,512]{2,1,0:T(8,128)(2,1)S(1)}, bf16[10,512,512]{2,1,0:T(8,128)(2,1)}, u32[]{:S(2)}) copy-start(bf16[10,512,512]{2,1,0:T(8,128)(2,1)} %left.3) | copy-start | bytes 15728644
  94.5 1.2 copy-start.6
  95.7 7.0 %copy-start.1 = (bf16[20,512,256]{2,1,0:T(8,128)(2,1)S(1)}, bf16[20,512,256]{2,1,0:T(8,128)(2,1)}, u32[]{:S(2)}) copy-start(bf16[20,512,256]{2,1,0:T(8,128)(2,1)} %copy-done) | copy-start | bytes 15728644
  102.6 2.5 %copy-start.2 = (bf16[10,512,512]{2,1,0:T(8,128)(2,1)S(1)}, bf16[10,512,512]{2,1,0:T(8,128)(2,1)}, u32[]{:S(2)}) copy-start(bf16[10,512,512]{2,1,0:T(8,128)(2,1)} %refs_5_.7) | copy-start | bytes 15728644
  110.6 7.2 %collective-permute-start.4 = (bf16[2,128,512]{2,1,0:T(8,128)(2,1)S(1)}, bf16[2,128,512]{2,1,0:T(8,128)(2,1)S(1)}, u32[]{:S(2)}, u32[]{:S(2)}) collective-permute-start(bf16[2,128,512]{2,1,0:T(8,128)(2,1)S(1)} %bitcast.27), channel_id=1, source_target_pairs={{0,2},{1,3},{2,0},{3,1},{4,6},{5,7},{6,4},{7,5},{8,10},{9,11},{10,... | collective-permute-start | bytes 786440 | tf_op jit(solution)/shard_map/ppermute | solution.py:150
  114.1 13.2 %collective-permute-start.6 = (bf16[2,128,512]{2,1,0:T(8,128)(2,1)S(1)}, bf16[2,128,512]{2,1,0:T(8,128)(2,1)S(1)}, u32[]{:S(2)}, u32[]{:S(2)}) collective-permute-start(bf16[2,128,512]{2,1,0:T(8,128)(2,1)S(1)} %bitcast.24), channel_id=1, source_target_pairs={{0,2},{1,3},{2,0},{3,1},{4,6},{5,7},{6,4},{7,5},{8,10},{9,11},{10,... | collective-permute-start | bytes 786440 | tf_op jit(solution)/shard_map/ppermute | solution.py:150
  121.3 5.8 %collective-permute-start.9 = (bf16[2,128,512]{2,1,0:T(8,128)(2,1)S(1)}, bf16[2,128,512]{2,1,0:T(8,128)(2,1)S(1)}, u32[]{:S(2)}, u32[]{:S(2)}) collective-permute-start(bf16[2,128,512]{2,1,0:T(8,128)(2,1)S(1)} %bitcast.26), channel_id=1, source_target_pairs={{0,2},{1,3},{2,0},{3,1},{4,6},{5,7},{6,4},{7,5},{8,10},{9,11},{10,... | collective-permute-start | bytes 786440 | tf_op jit(solution)/shard_map/ppermute | solution.py:150
  121.8 5.4 %collective-permute-start.7 = (bf16[2,128,512]{2,1,0:T(8,128)(2,1)S(1)}, bf16[2,128,512]{2,1,0:T(8,128)(2,1)S(1)}, u32[]{:S(2)}, u32[]{:S(2)}) collective-permute-start(bf16[2,128,512]{2,1,0:T(8,128)(2,1)S(1)} %add_convert_fusion.2), channel_id=1, source_target_pairs={{0,4},{1,5},{2,6},{3,7},{4,0},{5,1},{6,2},{7,3},{8,12},{9,13},{10,... | collective-permute-start | bytes 786440 | tf_op jit(solution)/shard_map/ppermute | solution.py:150
  123.9 8.7 %collective-permute-start.5 = (bf16[2,128,512]{2,1,0:T(8,128)(2,1)S(1)}, bf16[2,128,512]{2,1,0:T(8,128)(2,1)S(1)}, u32[]{:S(2)}, u32[]{:S(2)}) collective-permute-start(bf16[2,128,512]{2,1,0:T(8,128)(2,1)S(1)} %bitcast.25), channel_id=1, source_target_pairs={{0,2},{1,3},{2,0},{3,1},{4,6},{5,7},{6,4},{7,5},{8,10},{9,11},{10,... | collective-permute-start | bytes 786440 | tf_op jit(solution)/shard_map/ppermute | solution.py:150
  127.2 6.5 %collective-permute-start.10 = (bf16[2,128,512]{2,1,0:T(8,128)(2,1)S(1)}, bf16[2,128,512]{2,1,0:T(8,128)(2,1)S(1)}, u32[]{:S(2)}, u32[]{:S(2)}) collective-permute-start(bf16[2,128,512]{2,1,0:T(8,128)(2,1)S(1)} %add_convert_fusion), channel_id=1, source_target_pairs={{0,4},{1,5},{2,6},{3,7},{4,0},{5,1},{6,2},{7,3},{8,12},{9,13},{10,... | collective-permute-start | bytes 786440 | tf_op jit(solution)/shard_map/ppermute | solution.py:150
  127.4 6.7 %collective-permute-start.8 = (bf16[2,128,512]{2,1,0:T(8,128)(2,1)S(1)}, bf16[2,128,512]{2,1,0:T(8,128)(2,1)S(1)}, u32[]{:S(2)}, u32[]{:S(2)}) collective-permute-start(bf16[2,128,512]{2,1,0:T(8,128)(2,1)S(1)} %add_convert_fusion.1), channel_id=1, source_target_pairs={{0,12},{1,13},{2,14},{3,15},{4,8},{5,9},{6,10},{7,11},{8,4},{9,5},... | collective-permute-start | bytes 786440 | tf_op jit(solution)/shard_map/ppermute | solution.py:150
  134.3 10.3 %collective-permute-start.11 = (f32[128,512]{1,0:T(8,128)S(1)}, f32[128,512]{1,0:T(8,128)S(1)}, u32[]{:S(2)}, u32[]{:S(2)}) collective-permute-start(f32[128,512]{1,0:T(8,128)S(1)} %slice_bitcast_fusion), channel_id=1, source_target_pairs={{0,1},{1,0},{2,3},{3,2},{4,5},{5,4},{6,7},{7,6},{8,9},{9,8},{10,11... | collective-permute-start | bytes 786440 | tf_op jit(solution)/shard_map/ppermute | solution.py:150
Sparse Core Ops, SparseCore 0:
  11.5 39.2 all-gather.2
  53.0 38.9 all-gather.4

commit v4 on v2

v4 whole, which is shorter than its diff:
```python
import functools

import jax
import jax.numpy as jnp
from jax import lax
from jax.experimental import pallas as pl
from jax.experimental.pallas import tpu as pltpu
from jax.sharding import PartitionSpec as P

F32, BF16 = jnp.float32, jnp.bfloat16
CORES = 2
VMEM = 24 * 1024 * 1024
ANY = pl.BlockSpec(memory_space=pl.ANY)
SMEM = pl.BlockSpec(memory_space=pltpu.SMEM)
WHOLE = pl.BlockSpec(memory_space=pltpu.VMEM)


def list_slots(own, sib, field, sector, slots, found):
    count = jnp.int32(0)
    for core, meta in enumerate((own, sib)):
        live = meta[2 * slots]
        for t in range(slots):
            found[count] = core * slots + t
            hit = jnp.logical_and(t < live, meta[field * slots + t] == sector)
            count = count + hit.astype(jnp.int32)
    return count


def in_pairs(count, depth, fetch, wait, work):
    for i in range(depth - 2):
        @pl.when(i < count)
        def _():
            fetch(i, i)

    def pair(p, carry):
        i = 2 * p
        for ahead in (i + depth - 2, i + depth - 1):
            @pl.when(ahead < count)
            def _():
                fetch(ahead, lax.rem(ahead, depth))
        spots = [lax.rem(i, depth), lax.rem(i, depth) + 1]
        for k in spots:
            wait(k)
        work((i, i + 1), spots)
        return carry

    lax.fori_loop(0, count // 2, pair, 0)

    @pl.when(count % 2 == 1)
    def _():
        k = lax.rem(count - 1, depth)
        wait(k)
        work((count - 1,), (k,))


def start_fetch(term, slots, own_hbm, sib_hbm, target, sem):
    @pl.when(term < slots)
    def _():
        pltpu.make_async_copy(own_hbm.at[term], target, sem).start()

    @pl.when(term >= slots)
    def _():
        pltpu.make_async_copy(sib_hbm.at[term - slots], target, sem).start()


def left_kernel(phase, *refs):
    (own, sib, where, here, others, left, left_sib), refs = refs[:7], refs[7:]
    mixed, found, source, lbuf, obuf, lsem, osem = refs[-7:]
    slots, depth, outs = left.shape[0], lbuf.shape[0], obuf.shape[0]
    half = here.shape[1]
    bands = others.shape[0] + 1
    sector, band, core = where[phase], where[where.shape[0] - 2], where[where.shape[0] - 1]
    count = list_slots(own, sib, 0, sector, slots, found)

    def fetch(i, k):
        start_fetch(found[i], slots, left, left_sib, lbuf.at[k], lsem.at[k])

    def wait(k):
        pltpu.make_async_copy(left.at[0], lbuf.at[k], lsem.at[k]).wait()

    def out_copy(i, o):
        return pltpu.make_async_copy(obuf.at[o], mixed.at[found[i]], osem.at[o])

    def work(items, spots):
        for i, k in zip(items, spots):
            o = lax.rem(i, outs)

            @pl.when(i >= outs)
            def _():
                out_copy(i - outs, o).wait()

            obuf[o] = jnp.dot(lbuf[k], source[...], preferred_element_type=F32).astype(BF16)
            out_copy(i, o).start()

    for j in range(bands):
        b = lax.rem(band + j, bands)
        for i in range(CORES):
            c = core if i == 0 else 1 - core
            row = pl.multiple_of((b * CORES + c) * half, half)
            source[pl.ds(row, half)] = here[i] if j == 0 else others[j - 1, i]
    in_pairs(count, depth, fetch, wait, work)
    for back in range(outs, 0, -1):
        @pl.when(count >= back)
        def _():
            out_copy(count - back, lax.rem(count - back, outs)).wait()


def right_kernel(phase, own, sib, where, mixed, right, right_sib, keep, send, found, acc, rbuf, rsem):
    slots, depth = right.shape[0], rbuf.shape[0]
    half = keep.shape[1]
    bands = send.shape[0] + 1
    sector, band, core = where[phase], where[where.shape[0] - 2], where[where.shape[0] - 1]
    count = list_slots(own, sib, 1, sector, slots, found)

    def fetch(i, k):
        start_fetch(found[i], slots, right, right_sib, rbuf.at[k], rsem.at[k])

    def wait(k):
        pltpu.make_async_copy(right.at[0], rbuf.at[k], rsem.at[k]).wait()

    def work(items, spots):
        acc[...] += sum(
            lax.dot_general(mixed[found[i]], rbuf[k], (((1,), (1,)), ((), ())), preferred_element_type=F32)
            for i, k in zip(items, spots)
        )

    acc[...] = jnp.zeros_like(acc)
    in_pairs(count, depth, fetch, wait, work)
    for j in range(bands):
        b = lax.rem(band + j, bands)
        for i in range(CORES):
            c = core if i == 0 else 1 - core
            rows = acc[pl.ds(pl.multiple_of((b * CORES + c) * half, half), half)]
            if j == 0:
                keep[i] = rows
            else:
                send[j - 1, i] = rows.astype(BF16)


def local(devices, wavefunction, left, right, src, dst, live):
    slots, width = left.shape[0], left.shape[1]
    half = wavefunction.shape[0]
    sectors = half * devices // width
    bands = devices // (sectors * CORES)
    assert sectors == 4
    me = lax.axis_index("term")
    core, band, plane = me % CORES, (me // CORES) % bands, me // (CORES * bands)

    def move(value, to_plane=lambda a: a, band_step=0, flip=False):
        pairs = []
        for i in range(devices):
            c, b, a = i % CORES, (i // CORES) % bands, i // (CORES * bands)
            c = 1 - c if flip else c
            pairs.append((i, (to_plane(a) * bands + (b + band_step) % bands) * CORES + c))
        return lax.ppermute(value, "term", pairs)

    def beside(a):
        return a ^ 1

    def mirror(a):
        return 3 - a

    def bands_of(block):
        return jnp.stack([move(block, band_step=-j) for j in range(1, bands)])

    own_meta = jnp.concatenate([src, dst, live])
    sib_meta = move(own_meta, flip=True)
    mine = lax.dynamic_slice_in_dim(wavefunction, core * width, width, 1)
    theirs = lax.dynamic_slice_in_dim(wavefunction, (1 - core) * width, width, 1)
    from_sib = move(theirs, flip=True)
    left_sib, from_sib = lax.optimization_barrier((left, from_sib))
    left_sib = move(left_sib, flip=True)
    own_block = jnp.stack([mine, from_sib])
    mirror_block = move(own_block, mirror)
    beside_block, own_bands = lax.optimization_barrier((move(own_block, beside), bands_of(own_block)))
    beside_bands = bands_of(beside_block)
    mirror_block, right_sib, beside_block, own_bands = lax.optimization_barrier(
        (mirror_block, right, beside_block, own_bands)
    )
    right_sib = move(right_sib, flip=True)
    mirror_bands = bands_of(mirror_block)
    far_block = move(mirror_block, beside)
    blocks = [
        (own_block, own_bands),
        (beside_block, beside_bands),
        (mirror_block, mirror_bands),
        (far_block, bands_of(far_block)),
    ]
    partner = plane ^ 1
    where_src = jnp.stack([plane, partner, 3 - plane, 3 - partner, band, core]).astype(jnp.int32)
    where_dst = jnp.stack([3 - partner, 3 - plane, partner, plane, band, core]).astype(jnp.int32)

    params = pltpu.CompilerParams(vmem_limit_bytes=VMEM)
    cost = pl.CostEstimate(flops=3 * 10**9, bytes_accessed=7 * width * width * 2, transcendentals=0)
    depth = 8
    mixed = None
    for phase in range(sectors):
        operands = [own_meta, sib_meta, where_src, *blocks[phase], left, left_sib]
        if mixed is not None:
            operands.append(mixed)
        mixed = pl.pallas_call(
            functools.partial(left_kernel, phase),
            out_shape=jax.ShapeDtypeStruct((CORES * slots, width, width), BF16),
            in_specs=[SMEM] * 3 + [WHOLE] * 2 + [ANY] * (len(operands) - 5),
            out_specs=ANY,
            scratch_shapes=[
                pltpu.SMEM((CORES * slots + 1,), jnp.int32),
                pltpu.VMEM((width, width), BF16),
                pltpu.VMEM((depth, width, width), BF16),
                pltpu.VMEM((4, width, width), BF16),
                pltpu.SemaphoreType.DMA((depth,)),
                pltpu.SemaphoreType.DMA((4,)),
            ],
            input_output_aliases={} if mixed is None else {7: 0},
            compiler_params=params,
            cost_estimate=cost,
            name="left_mix",
        )(*operands)

    def right_mix(phase, meta):
        keep, send = pl.pallas_call(
            functools.partial(right_kernel, phase),
            out_shape=(
                jax.ShapeDtypeStruct((CORES, half, width), F32),
                jax.ShapeDtypeStruct((bands - 1, CORES, half, width), BF16),
            ),
            in_specs=[SMEM] * 3 + [WHOLE] + [ANY] * 2,
            out_specs=(WHOLE, WHOLE),
            scratch_shapes=[
                pltpu.SMEM((CORES * slots + 1,), jnp.int32),
                pltpu.VMEM((width, width), F32),
                pltpu.VMEM((depth, width, width), BF16),
                pltpu.SemaphoreType.DMA((depth,)),
            ],
            compiler_params=params,
            cost_estimate=cost,
            name="right_mix",
        )(meta, sib_meta, where_dst, mixed, right, right_sib)
        for j in range(1, bands):
            keep = keep + move(send[j - 1], band_step=j).astype(F32)
        return keep

    beside_far = right_mix(0, own_meta).astype(BF16)
    mirrored = right_mix(1, own_meta)
    meta, beside_far = lax.optimization_barrier((own_meta, beside_far))
    mirrored = (mirrored + move(beside_far, beside).astype(F32)).astype(BF16)
    beside_near = right_mix(2, meta).astype(BF16)
    total = right_mix(3, meta) + move(mirrored, mirror).astype(F32) + move(beside_near, beside).astype(F32)
    same, cross = total[0], move(total[1], flip=True)
    first = core == 0
    return jnp.concatenate([jnp.where(first, same, cross), jnp.where(first, cross, same)], axis=1)


def solution(mesh):
    spec = P(("parts", "term"))
    return jax.shard_map(
        functools.partial(local, mesh.shape["term"]),
        mesh=mesh,
        in_specs=(spec,) * 6,
        out_specs=spec,
        check_vma=False,
    )
```

time: 94.8 us -> 85.5 us (0.902)
  the two profiles are of different devices: /device:TPU:0 before, /device:TPU:13 now
where the time goes in v4:
time: 85.5 us; the launch traced here: 85.3 us
  waiting for transfers between devices  31.3 us (37%)
  starting transfers between devices  29.9 us (35%)
  Pallas kernels  17.6 us (21%)
  local copies, waits for them, and re-layouts  3.67 us (4%)
  other arithmetic  2.02 us (2%)
    ppermute x19, waiting for transfers between devices, move(): return lax.ppermute(value, 'term', pairs)  31.3 us
    ppermute x19, starting transfers between devices, move(): return lax.ppermute(value, 'term', pairs)  29.9 us
    pallas_call x4, Pallas kernels, local(): pl.pallas_call(functools.partial(left_kernel, phase), out_shape=jax.Shape...  8.81 us
    pallas_call x4, Pallas kernels, right_mix(): pl.pallas_call(functools.partial(right_kernel, phase), out_shape=(jax.Sha...  8.74 us
    unnamed x6, local copies, waits for them, and re-layouts  2.5 us
  transfers between devices with their start and end apart: 19, of which 11 were waited for; matrix products, arithmetic and copies ran while one was open for 1% of the time, Pallas kernels for 18%

profile of v4, /device:TPU:13, one launch (start us, length us, event | category | flops | bytes accessed | tf_op | source)
XLA Modules:
  0.0 85.3 jit_solution(14297417774116220156)
XLA Ops:
  0.0 1.0 %dynamic-slice_bitcast_fusion = (bf16[1,128,512]{2,1,0:T(8,128)(2,1)S(1)}, bf16[128,512]{1,0:T(8,128)(2,1)S(1)}) fusion(bf16[128,1024]{1,0:T(8,128)(2,1)} %param.6, s32[]{:T(128)S(6)} %select_n.41, s32[]{:T(128)S(6)} %select_n.42), kind=kLoop, calls=%fused_computation.10 | loop fusion | bytes 524296 | tf_op jit(solution)/shard_map/stack | solution.py:173
  1.0 0.7 collective-permute-start.1
  1.7 1.0 %collective-permute-done.1 = bf16[128,512]{1,0:T(8,128)(2,1)S(1)} collective-permute-done((bf16[128,512]{1,0:T(8,128)(2,1)S(1)}, bf16[128,512]{1,0:T(8,128)(2,1)S(1)}, u32[]{:S(2)}, u32[]{:S(2)}) %collective-permute-start.1) | collective-permute-done | bytes 131104 | tf_op jit(solution)/shard_map/ppermute | solution.py:155
  2.7 0.4 collective-permute-start.7
  3.1 1.3 %collective-permute-start.4 = (bf16[2,128,512]{2,1,0:T(8,128)(2,1)S(1)}, bf16[2,128,512]{2,1,0:T(8,128)(2,1)S(1)}, u32[]{:S(2)}, u32[]{:S(2)}) collective-permute-start(bf16[2,128,512]{2,1,0:T(8,128)(2,1)S(1)} %pad_maximum_fusion.1.refs_3_), channel_id=1, source_target_pairs={{0,2},{1,3},{2,0},{3,1},{4,6},{5,7},{6,4},{7,5},{8,10},{9,11},{10,... | collective-permute-start | bytes 786440 | tf_op jit(solution)/shard_map/ppermute | solution.py:155
  4.4 0.2 collective-permute-start.3
  4.6 2.4 %collective-permute-start.2 = (bf16[2,128,512]{2,1,0:T(8,128)(2,1)S(1)}, bf16[2,128,512]{2,1,0:T(8,128)(2,1)S(1)}, u32[]{:S(2)}, u32[]{:S(2)}) collective-permute-start(bf16[2,128,512]{2,1,0:T(8,128)(2,1)S(1)} %pad_maximum_fusion.1.refs_3_), channel_id=1, source_target_pairs={{0,12},{1,13},{2,14},{3,15},{4,8},{5,9},{6,10},{7,11},{8,4},{9,5},... | collective-permute-start | bytes 786440 | tf_op jit(solution)/shard_map/ppermute | solution.py:155
  7.0 4.0 %collective-permute-done.4 = bf16[2,128,512]{2,1,0:T(8,128)(2,1)S(1)} collective-permute-done((bf16[2,128,512]{2,1,0:T(8,128)(2,1)S(1)}, bf16[2,128,512]{2,1,0:T(8,128)(2,1)S(1)}, u32[]{:S(2)}, u32[]{:S(2)}) %collective-permute-start.4) | collective-permute-done | bytes 262176 | tf_op jit(solution)/shard_map/ppermute | solution.py:155
  10.9 0.9 %collective-permute-done.3.refs_3_ = bf16[2,128,512]{2,1,0:T(8,128)(2,1)S(1)} collective-permute-done((bf16[2,128,512]{2,1,0:T(8,128)(2,1)S(1)}, bf16[2,128,512]{2,1,0:T(8,128)(2,1)S(1)}, u32[]{:S(2)}, u32[]{:S(2)}) %collective-permute-start.3) | collective-permute-done | bytes 262176 | tf_op jit(solution)/shard_map/ppermute | solution.py:155
  11.8 1.2 %collective-permute-done.2.refs_3_ = bf16[2,128,512]{2,1,0:T(8,128)(2,1)S(1)} collective-permute-done((bf16[2,128,512]{2,1,0:T(8,128)(2,1)S(1)}, bf16[2,128,512]{2,1,0:T(8,128)(2,1)S(1)}, u32[]{:S(2)}, u32[]{:S(2)}) %collective-permute-start.2) | collective-permute-done | bytes 262176 | tf_op jit(solution)/shard_map/ppermute | solution.py:155
  13.1 6.8 %collective-permute-start.10 = (bf16[10,512,512]{2,1,0:T(8,128)(2,1)}, bf16[10,512,512]{2,1,0:T(8,128)(2,1)}, u32[]{:S(2)}, u32[]{:S(2)}) collective-permute-start(bf16[10,512,512]{2,1,0:T(8,128)(2,1)} %right.7), channel_id=1, source_target_pairs={{0,1},{1,0},{2,3},{3,2},{4,5},{5,4},{6,7},{7,6},{8,9},{9,8},{10,11... | collective-permute-start | bytes 15728648 | tf_op jit(solution)/shard_map/ppermute | solution.py:155
  19.9 1.2 %collective-permute-start.5 = (bf16[2,128,512]{2,1,0:T(8,128)(2,1)S(1)}, bf16[2,128,512]{2,1,0:T(8,128)(2,1)S(1)}, u32[]{:S(2)}, u32[]{:S(2)}) collective-permute-start(bf16[2,128,512]{2,1,0:T(8,128)(2,1)S(1)} %collective-permute-done.2.refs_3_), channel_id=1, source_target_pairs={{0,4},{1,5},{2,6},{3,7},{4,0},{5,1},{6,2},{7,3},{8,12},{9,13},{10,... | collective-permute-start | bytes 786440 | tf_op jit(solution)/shard_map/ppermute | solution.py:155
  21.7 0.7 pad_add_fusion.refs_0_.own
  22.4 0.3 collective-permute-start
  22.7 0.1 stack.58.refs_2_
  22.8 0.1 stack.57.where
  22.9 0.3 collective-permute-start.9
  23.1 5.0 %collective-permute-done.refs_1_.sib = s32[21]{0:T(128)S(1)} collective-permute-done((s32[21]{0:T(128)S(1)}, s32[21]{0:T(128)S(1)}, u32[]{:S(2)}, u32[]{:S(2)}) %collective-permute-start) | collective-permute-done | bytes 116 | tf_op jit(solution)/shard_map/ppermute | solution.py:155
  28.1 0.3 collective-permute-start.8
  28.4 0.0 collective-permute-done.5.refs_3_
  28.4 1.2 %collective-permute-start.6 = (bf16[2,128,512]{2,1,0:T(8,128)(2,1)S(1)}, bf16[2,128,512]{2,1,0:T(8,128)(2,1)S(1)}, u32[]{:S(2)}, u32[]{:S(2)}) collective-permute-start(bf16[2,128,512]{2,1,0:T(8,128)(2,1)S(1)} %collective-permute-done.5.refs_3_), channel_id=1, source_target_pairs={{0,2},{1,3},{2,0},{3,1},{4,6},{5,7},{6,4},{7,5},{8,10},{9,11},{10,... | collective-permute-start | bytes 786440 | tf_op jit(solution)/shard_map/ppermute | solution.py:155
  29.6 0.0 collective-permute-done.7.refs_6_
  29.6 0.0 copy-start
  29.6 2.5 %copy-done = bf16[10,512,512]{2,1,0:T(8,128)(2,1)S(1)} copy-done((bf16[10,512,512]{2,1,0:T(8,128)(2,1)S(1)}, bf16[10,512,512]{2,1,0:T(8,128)(2,1)}, u32[]{:S(2)}) %copy-start) | copy-done | bytes 5242904
  32.1 1.3 %left_mix.4.refs_7_ = bf16[20,512,512]{2,1,0:T(8,128)(2,1)S(1)} custom-call(s32[21]{0:T(128)S(1)} %pad_add_fusion.refs_0_.own, s32[21]{0:T(128)S(1)} %collective-permute-done.refs_1_.sib, s32[6]{0:T(128)S(1)} %stack.58.refs_2_, bf16[2,128,512]{2,1,0:T(8,128)(2,1)S(1)} %pad_maximum_fusion.1.refs_3_, bf16[1,2,128,512]{3,2,1,0:T(8,128)(2,1)S(1)} %bitcast.27, ...), custom_call_target="tpu_custom_call" | custom-call | flops 3000000000 | bytes 3670016 | tf_op jit(solution)/shard_map/left_mix/pallas_call | solution.py:201
  33.4 0.0 collective-permute-done.9
  33.4 1.3 %left_mix.5.refs_7_ = bf16[20,512,512]{2,1,0:T(8,128)(2,1)S(1)} custom-call(s32[21]{0:T(128)S(1)} %pad_add_fusion.refs_0_.own, s32[21]{0:T(128)S(1)} %collective-permute-done.refs_1_.sib, s32[6]{0:T(128)S(1)} %stack.58.refs_2_, bf16[2,128,512]{2,1,0:T(8,128)(2,1)S(1)} %collective-permute-done.3.refs_3_, ...), custom_call_target="tpu_custom_call", output_to_operand_aliasing={{}: (7, {})} | custom-call | flops 3000000000 | bytes 3670016 | tf_op jit(solution)/shard_map/left_mix/pallas_call | solution.py:201
  34.8 1.6 %collective-permute-done.8 = bf16[2,128,512]{2,1,0:T(8,128)(2,1)S(1)} collective-permute-done((bf16[2,128,512]{2,1,0:T(8,128)(2,1)S(1)}, bf16[2,128,512]{2,1,0:T(8,128)(2,1)S(1)}, u32[]{:S(2)}, u32[]{:S(2)}) %collective-permute-start.8) | collective-permute-done | bytes 262176 | tf_op jit(solution)/shard_map/ppermute | solution.py:155
  36.4 0.0 slice-start
  36.4 3.2 %left_mix.6.refs_7_ = bf16[20,512,512]{2,1,0:T(8,128)(2,1)S(1)} custom-call(s32[21]{0:T(128)S(1)} %pad_add_fusion.refs_0_.own, s32[21]{0:T(128)S(1)} %collective-permute-done.refs_1_.sib, s32[6]{0:T(128)S(1)} %stack.58.refs_2_, bf16[2,128,512]{2,1,0:T(8,128)(2,1)S(1)} %collective-permute-done.2.refs_3_, ...), custom_call_target="tpu_custom_call", output_to_operand_aliasing={{}: (7, {})} | custom-call | flops 3000000000 | bytes 3670016 | tf_op jit(solution)/shard_map/left_mix/pallas_call | solution.py:201
  39.7 0.0 slice-start.1
  39.7 2.3 %collective-permute-done.6 = bf16[2,128,512]{2,1,0:T(8,128)(2,1)S(1)} collective-permute-done((bf16[2,128,512]{2,1,0:T(8,128)(2,1)S(1)}, bf16[2,128,512]{2,1,0:T(8,128)(2,1)S(1)}, u32[]{:S(2)}, u32[]{:S(2)}) %collective-permute-start.6) | collective-permute-done | bytes 262176 | tf_op jit(solution)/shard_map/ppermute | solution.py:155
  42.0 2.9 %left_mix.7.mixed = bf16[20,512,512]{2,1,0:T(8,128)(2,1)S(1)} custom-call(s32[21]{0:T(128)S(1)} %pad_add_fusion.refs_0_.own, s32[21]{0:T(128)S(1)} %collective-permute-done.refs_1_.sib, s32[6]{0:T(128)S(1)} %stack.58.refs_2_, bf16[2,128,512]{2,1,0:T(8,128)(2,1)S(1)} %collective-permute-done.5.refs_3_, ...), custom_call_target="tpu_custom_call", output_to_operand_aliasing={{}: (7, {})} | custom-call | flops 3000000000 | bytes 3670016 | tf_op jit(solution)/shard_map/left_mix/pallas_call | solution.py:201
  45.0 0.0 collective-permute-done.10.right_sib
  45.0 0.0 slice-done
  45.0 0.0 slice-done.1
  45.0 2.3 %right_mix.4 = (f32[2,128,512]{2,1,0:T(8,128)S(1)}, bf16[1,2,128,512]{3,2,1,0:T(8,128)(2,1)S(1)}) custom-call(s32[21]{0:T(128)S(1)} %pad_add_fusion.refs_0_.own, s32[21]{0:T(128)S(1)} %collective-permute-done.refs_1_.sib, s32[6]{0:T(128)S(1)} %stack.57.where, bf16[20,512,512]{2,1,0:T(8,128)(2,1)S(1)} %left_mix.7.mixed, bf16[10,512,512]{2,1,0:T(8,128)(2,1)S(1)} %bitcast.26, ...), custom_call_target="tpu_custom_call" | custom-call | flops 3000000000 | bytes 3670016 | tf_op jit(solution)/shard_map/right_mix/pallas_call | solution.py:221
  47.3 0.3 collective-permute-start.11
  47.5 2.1 %right_mix.6 = (f32[2,128,512]{2,1,0:T(8,128)S(1)}, bf16[1,2,128,512]{3,2,1,0:T(8,128)(2,1)S(1)}) custom-call(s32[21]{0:T(128)S(1)} %pad_add_fusion.refs_0_.own, s32[21]{0:T(128)S(1)} %collective-permute-done.refs_1_.sib, s32[6]{0:T(128)S(1)} %stack.57.where, bf16[20,512,512]{2,1,0:T(8,128)(2,1)S(1)} %left_mix.7.mixed, bf16[10,512,512]{2,1,0:T(8,128)(2,1)S(1)} %bitcast.26, ...), custom_call_target="tpu_custom_call" | custom-call | flops 3000000000 | bytes 3670016 | tf_op jit(solution)/shard_map/right_mix/pallas_call | solution.py:221
  49.7 2.4 %collective-permute-start.13 = (bf16[2,128,512]{2,1,0:T(8,128)(2,1)S(1)}, bf16[2,128,512]{2,1,0:T(8,128)(2,1)S(1)}, u32[]{:S(2)}, u32[]{:S(2)}) collective-permute-start(bf16[2,128,512]{2,1,0:T(8,128)(2,1)S(1)} %bitcast.32), channel_id=1, source_target_pairs={{0,2},{1,3},{2,0},{3,1},{4,6},{5,7},{6,4},{7,5},{8,10},{9,11},{10,... | collective-permute-start | bytes 786440 | tf_op jit(solution)/shard_map/ppermute | solution.py:155
  52.1 2.4 %collective-permute-done.11 = bf16[2,128,512]{2,1,0:T(8,128)(2,1)S(1)} collective-permute-done((bf16[2,128,512]{2,1,0:T(8,128)(2,1)S(1)}, bf16[2,128,512]{2,1,0:T(8,128)(2,1)S(1)}, u32[]{:S(2)}, u32[]{:S(2)}) %collective-permute-start.11) | collective-permute-done | bytes 262176 | tf_op jit(solution)/shard_map/ppermute | solution.py:155
  54.5 0.1 add_convert_fusion.2
  54.5 0.1 collective-permute-start.14
  54.6 2.7 %right_mix.7 = (f32[2,128,512]{2,1,0:T(8,128)S(1)}, bf16[1,2,128,512]{3,2,1,0:T(8,128)(2,1)S(1)}) custom-call(s32[21]{0:T(128)S(1)} %pad_add_fusion.refs_0_.own, s32[21]{0:T(128)S(1)} %collective-permute-done.refs_1_.sib, s32[6]{0:T(128)S(1)} %stack.57.where, bf16[20,512,512]{2,1,0:T(8,128)(2,1)S(1)} %left_mix.7.mixed, bf16[10,512,512]{2,1,0:T(8,128)(2,1)S(1)} %bitcast.26, ...), custom_call_target="tpu_custom_call" | custom-call | flops 3000000000 | bytes 3670016 | tf_op jit(solution)/shard_map/right_mix/pallas_call | solution.py:221
  57.3 1.4 %collective-permute-start.16 = (bf16[2,128,512]{2,1,0:T(8,128)(2,1)S(1)}, bf16[2,128,512]{2,1,0:T(8,128)(2,1)S(1)}, u32[]{:S(2)}, u32[]{:S(2)}) collective-permute-start(bf16[2,128,512]{2,1,0:T(8,128)(2,1)S(1)} %bitcast.33), channel_id=1, source_target_pairs={{0,2},{1,3},{2,0},{3,1},{4,6},{5,7},{6,4},{7,5},{8,10},{9,11},{10,... | collective-permute-start | bytes 786440 | tf_op jit(solution)/shard_map/ppermute | solution.py:155
  58.7 1.6 %right_mix.5 = (f32[2,128,512]{2,1,0:T(8,128)S(1)}, bf16[1,2,128,512]{3,2,1,0:T(8,128)(2,1)S(1)}) custom-call(s32[21]{0:T(128)S(1)} %pad_add_fusion.refs_0_.own, s32[21]{0:T(128)S(1)} %collective-permute-done.refs_1_.sib, s32[6]{0:T(128)S(1)} %stack.57.where, bf16[20,512,512]{2,1,0:T(8,128)(2,1)S(1)} %left_mix.7.mixed, bf16[10,512,512]{2,1,0:T(8,128)(2,1)S(1)} %bitcast.26, ...), custom_call_target="tpu_custom_call" | custom-call | flops 3000000000 | bytes 3670016 | tf_op jit(solution)/shard_map/right_mix/pallas_call | solution.py:221
  60.3 1.6 %collective-permute-start.12 = (bf16[2,128,512]{2,1,0:T(8,128)(2,1)S(1)}, bf16[2,128,512]{2,1,0:T(8,128)(2,1)S(1)}, u32[]{:S(2)}, u32[]{:S(2)}) collective-permute-start(bf16[2,128,512]{2,1,0:T(8,128)(2,1)S(1)} %bitcast.31), channel_id=1, source_target_pairs={{0,2},{1,3},{2,0},{3,1},{4,6},{5,7},{6,4},{7,5},{8,10},{9,11},{10,... | collective-permute-start | bytes 786440 | tf_op jit(solution)/shard_map/ppermute | solution.py:155
  62.0 0.0 collective-permute-done.13
  62.0 0.0 collective-permute-done.14
  62.0 0.1 add_convert_fusion.1
  62.1 5.8 %collective-permute-start.15 = (bf16[2,128,512]{2,1,0:T(8,128)(2,1)S(1)}, bf16[2,128,512]{2,1,0:T(8,128)(2,1)S(1)}, u32[]{:S(2)}, u32[]{:S(2)}) collective-permute-start(bf16[2,128,512]{2,1,0:T(8,128)(2,1)S(1)} %add_convert_fusion.1), channel_id=1, source_target_pairs={{0,12},{1,13},{2,14},{3,15},{4,8},{5,9},{6,10},{7,11},{8,4},{9,5},... | collective-permute-start | bytes 786440 | tf_op jit(solution)/shard_map/ppermute | solution.py:155
  67.9 0.0 collective-permute-done.16
  67.9 0.1 add_convert_fusion
  68.0 3.1 %collective-permute-start.17 = (bf16[2,128,512]{2,1,0:T(8,128)(2,1)S(1)}, bf16[2,128,512]{2,1,0:T(8,128)(2,1)S(1)}, u32[]{:S(2)}, u32[]{:S(2)}) collective-permute-start(bf16[2,128,512]{2,1,0:T(8,128)(2,1)S(1)} %add_convert_fusion), channel_id=1, source_target_pairs={{0,4},{1,5},{2,6},{3,7},{4,0},{5,1},{6,2},{7,3},{8,12},{9,13},{10,... | collective-permute-start | bytes 786440 | tf_op jit(solution)/shard_map/ppermute | solution.py:155
  71.1 0.0 collective-permute-done.12
  71.1 8.6 %collective-permute-done.15 = bf16[2,128,512]{2,1,0:T(8,128)(2,1)S(1)} collective-permute-done((bf16[2,128,512]{2,1,0:T(8,128)(2,1)S(1)}, bf16[2,128,512]{2,1,0:T(8,128)(2,1)S(1)}, u32[]{:S(2)}, u32[]{:S(2)}) %collective-permute-start.15) | collective-permute-done | bytes 262176 | tf_op jit(solution)/shard_map/ppermute | solution.py:155
  79.6 3.1 %collective-permute-done.17 = bf16[2,128,512]{2,1,0:T(8,128)(2,1)S(1)} collective-permute-done((bf16[2,128,512]{2,1,0:T(8,128)(2,1)S(1)}, bf16[2,128,512]{2,1,0:T(8,128)(2,1)S(1)}, u32[]{:S(2)}, u32[]{:S(2)}) %collective-permute-start.17) | collective-permute-done | bytes 262176 | tf_op jit(solution)/shard_map/ppermute | solution.py:155
  82.7 0.1 convert_add_fusion
  82.9 0.3 collective-permute-start.18
  83.2 1.3 %collective-permute-done.18 = f32[128,512]{1,0:T(8,128)S(1)} collective-permute-done((f32[128,512]{1,0:T(8,128)S(1)}, f32[128,512]{1,0:T(8,128)S(1)}, u32[]{:S(2)}, u32[]{:S(2)}) %collective-permute-start.18) | collective-permute-done | bytes 262176 | tf_op jit(solution)/shard_map/ppermute | solution.py:155
  84.5 0.8 pad_maximum_fusion
  (4 shorter events, 0.1 us)
Async XLA Ops:
  1.0 1.7 %collective-permute-start.1 = (bf16[128,512]{1,0:T(8,128)(2,1)S(1)}, bf16[128,512]{1,0:T(8,128)(2,1)S(1)}, u32[]{:S(2)}, u32[]{:S(2)}) collective-permute-start(bf16[128,512]{1,0:T(8,128)(2,1)S(1)} %get-tuple-element.44), channel_id=1, source_target_pairs={{0,1},{1,0},{2,3},{3,2},{4,5},{5,4},{6,7},{7,6},{8,9},{9,8},{10,11... | collective-permute-start | bytes 393224 | tf_op jit(solution)/shard_map/ppermute | solution.py:155
  2.7 26.9 %collective-permute-start.7 = (bf16[10,512,512]{2,1,0:T(8,128)(2,1)}, bf16[10,512,512]{2,1,0:T(8,128)(2,1)}, u32[]{:S(2)}, u32[]{:S(2)}) collective-permute-start(bf16[10,512,512]{2,1,0:T(8,128)(2,1)} %refs_5_.7), channel_id=1, source_target_pairs={{0,1},{1,0},{2,3},{3,2},{4,5},{5,4},{6,7},{7,6},{8,9},{9,8},{10,11... | collective-permute-start | bytes 15728648 | tf_op jit(solution)/shard_map/ppermute | solution.py:155
  3.1 7.8 %collective-permute-start.4 = (bf16[2,128,512]{2,1,0:T(8,128)(2,1)S(1)}, bf16[2,128,512]{2,1,0:T(8,128)(2,1)S(1)}, u32[]{:S(2)}, u32[]{:S(2)}) collective-permute-start(bf16[2,128,512]{2,1,0:T(8,128)(2,1)S(1)} %pad_maximum_fusion.1.refs_3_), channel_id=1, source_target_pairs={{0,2},{1,3},{2,0},{3,1},{4,6},{5,7},{6,4},{7,5},{8,10},{9,11},{10,... | collective-permute-start | bytes 786440 | tf_op jit(solution)/shard_map/ppermute | solution.py:155
  4.4 7.4 %collective-permute-start.3 = (bf16[2,128,512]{2,1,0:T(8,128)(2,1)S(1)}, bf16[2,128,512]{2,1,0:T(8,128)(2,1)S(1)}, u32[]{:S(2)}, u32[]{:S(2)}) collective-permute-start(bf16[2,128,512]{2,1,0:T(8,128)(2,1)S(1)} %pad_maximum_fusion.1.refs_3_), channel_id=1, source_target_pairs={{0,4},{1,5},{2,6},{3,7},{4,0},{5,1},{6,2},{7,3},{8,12},{9,13},{10,... | collective-permute-start | bytes 786440 | tf_op jit(solution)/shard_map/ppermute | solution.py:155
  4.6 8.5 %collective-permute-start.2 = (bf16[2,128,512]{2,1,0:T(8,128)(2,1)S(1)}, bf16[2,128,512]{2,1,0:T(8,128)(2,1)S(1)}, u32[]{:S(2)}, u32[]{:S(2)}) collective-permute-start(bf16[2,128,512]{2,1,0:T(8,128)(2,1)S(1)} %pad_maximum_fusion.1.refs_3_), channel_id=1, source_target_pairs={{0,12},{1,13},{2,14},{3,15},{4,8},{5,9},{6,10},{7,11},{8,4},{9,5},... | collective-permute-start | bytes 786440 | tf_op jit(solution)/shard_map/ppermute | solution.py:155
  13.1 31.9 %collective-permute-start.10 = (bf16[10,512,512]{2,1,0:T(8,128)(2,1)}, bf16[10,512,512]{2,1,0:T(8,128)(2,1)}, u32[]{:S(2)}, u32[]{:S(2)}) collective-permute-start(bf16[10,512,512]{2,1,0:T(8,128)(2,1)} %right.7), channel_id=1, source_target_pairs={{0,1},{1,0},{2,3},{3,2},{4,5},{5,4},{6,7},{7,6},{8,9},{9,8},{10,11... | collective-permute-start | bytes 15728648 | tf_op jit(solution)/shard_map/ppermute | solution.py:155
  19.9 8.5 %collective-permute-start.5 = (bf16[2,128,512]{2,1,0:T(8,128)(2,1)S(1)}, bf16[2,128,512]{2,1,0:T(8,128)(2,1)S(1)}, u32[]{:S(2)}, u32[]{:S(2)}) collective-permute-start(bf16[2,128,512]{2,1,0:T(8,128)(2,1)S(1)} %collective-permute-done.2.refs_3_), channel_id=1, source_target_pairs={{0,4},{1,5},{2,6},{3,7},{4,0},{5,1},{6,2},{7,3},{8,12},{9,13},{10,... | collective-permute-start | bytes 786440 | tf_op jit(solution)/shard_map/ppermute | solution.py:155
  22.4 5.7 %collective-permute-start = (s32[21]{0:T(128)S(1)}, s32[21]{0:T(128)S(1)}, u32[]{:S(2)}, u32[]{:S(2)}) collective-permute-start(s32[21]{0:T(128)S(1)} %pad_add_fusion.refs_0_.own), channel_id=1, source_target_pairs={{0,1},{1,0},{2,3},{3,2},{4,5},{5,4},{6,7},{7,6},{8,9},{9,8},{10,11... | collective-permute-start | bytes 260 | tf_op jit(solution)/shard_map/ppermute | solution.py:155
  22.9 10.6 %collective-permute-start.9 = (bf16[2,128,512]{2,1,0:T(8,128)(2,1)S(1)}, bf16[2,128,512]{2,1,0:T(8,128)(2,1)S(1)}, u32[]{:S(2)}, u32[]{:S(2)}) collective-permute-start(bf16[2,128,512]{2,1,0:T(8,128)(2,1)S(1)} %collective-permute-done.3.refs_3_), channel_id=1, source_target_pairs={{0,2},{1,3},{2,0},{3,1},{4,6},{5,7},{6,4},{7,5},{8,10},{9,11},{10,... | collective-permute-start | bytes 786440 | tf_op jit(solution)/shard_map/ppermute | solution.py:155
  28.1 8.3 %collective-permute-start.8 = (bf16[2,128,512]{2,1,0:T(8,128)(2,1)S(1)}, bf16[2,128,512]{2,1,0:T(8,128)(2,1)S(1)}, u32[]{:S(2)}, u32[]{:S(2)}) collective-permute-start(bf16[2,128,512]{2,1,0:T(8,128)(2,1)S(1)} %collective-permute-done.2.refs_3_), channel_id=1, source_target_pairs={{0,2},{1,3},{2,0},{3,1},{4,6},{5,7},{6,4},{7,5},{8,10},{9,11},{10,... | collective-permute-start | bytes 786440 | tf_op jit(solution)/shard_map/ppermute | solution.py:155
  28.4 13.6 %collective-permute-start.6 = (bf16[2,128,512]{2,1,0:T(8,128)(2,1)S(1)}, bf16[2,128,512]{2,1,0:T(8,128)(2,1)S(1)}, u32[]{:S(2)}, u32[]{:S(2)}) collective-permute-start(bf16[2,128,512]{2,1,0:T(8,128)(2,1)S(1)} %collective-permute-done.5.refs_3_), channel_id=1, source_target_pairs={{0,2},{1,3},{2,0},{3,1},{4,6},{5,7},{6,4},{7,5},{8,10},{9,11},{10,... | collective-permute-start | bytes 786440 | tf_op jit(solution)/shard_map/ppermute | solution.py:155
  29.6 2.5 %copy-start = (bf16[10,512,512]{2,1,0:T(8,128)(2,1)S(1)}, bf16[10,512,512]{2,1,0:T(8,128)(2,1)}, u32[]{:S(2)}) copy-start(bf16[10,512,512]{2,1,0:T(8,128)(2,1)} %refs_5_.7) | copy-start | bytes 15728644
  36.4 8.5 %slice-start = ((s8[5242880]{0:T(1024)(128)(4,1)}), s8[4194304]{0:T(1024)(128)(4,1)S(1)}, s32[]{:S(2)}) async-start(s8[5242880]{0:T(1024)(128)(4,1)} %bitcast.25), calls=%async_computation | async-start | bytes 8388608
  39.7 5.3 %slice-start.1 = ((s8[5242880]{0:T(1024)(128)(4,1)}), s8[1048576]{0:T(1024)(128)(4,1)S(1)}, s32[]{:S(2)}) async-start(s8[5242880]{0:T(1024)(128)(4,1)} %bitcast.25), calls=%async_computation.1 | async-start | bytes 2097152
  47.3 7.2 %collective-permute-start.11 = (bf16[2,128,512]{2,1,0:T(8,128)(2,1)S(1)}, bf16[2,128,512]{2,1,0:T(8,128)(2,1)S(1)}, u32[]{:S(2)}, u32[]{:S(2)}) collective-permute-start(bf16[2,128,512]{2,1,0:T(8,128)(2,1)S(1)} %bitcast.34), channel_id=1, source_target_pairs={{0,2},{1,3},{2,0},{3,1},{4,6},{5,7},{6,4},{7,5},{8,10},{9,11},{10,... | collective-permute-start | bytes 786440 | tf_op jit(solution)/shard_map/ppermute | solution.py:155
  49.7 12.3 %collective-permute-start.13 = (bf16[2,128,512]{2,1,0:T(8,128)(2,1)S(1)}, bf16[2,128,512]{2,1,0:T(8,128)(2,1)S(1)}, u32[]{:S(2)}, u32[]{:S(2)}) collective-permute-start(bf16[2,128,512]{2,1,0:T(8,128)(2,1)S(1)} %bitcast.32), channel_id=1, source_target_pairs={{0,2},{1,3},{2,0},{3,1},{4,6},{5,7},{6,4},{7,5},{8,10},{9,11},{10,... | collective-permute-start | bytes 786440 | tf_op jit(solution)/shard_map/ppermute | solution.py:155
  54.5 7.5 %collective-permute-start.14 = (bf16[2,128,512]{2,1,0:T(8,128)(2,1)S(1)}, bf16[2,128,512]{2,1,0:T(8,128)(2,1)S(1)}, u32[]{:S(2)}, u32[]{:S(2)}) collective-permute-start(bf16[2,128,512]{2,1,0:T(8,128)(2,1)S(1)} %add_convert_fusion.2), channel_id=1, source_target_pairs={{0,4},{1,5},{2,6},{3,7},{4,0},{5,1},{6,2},{7,3},{8,12},{9,13},{10,... | collective-permute-start | bytes 786440 | tf_op jit(solution)/shard_map/ppermute | solution.py:155
  57.3 10.6 %collective-permute-start.16 = (bf16[2,128,512]{2,1,0:T(8,128)(2,1)S(1)}, bf16[2,128,512]{2,1,0:T(8,128)(2,1)S(1)}, u32[]{:S(2)}, u32[]{:S(2)}) collective-permute-start(bf16[2,128,512]{2,1,0:T(8,128)(2,1)S(1)} %bitcast.33), channel_id=1, source_target_pairs={{0,2},{1,3},{2,0},{3,1},{4,6},{5,7},{6,4},{7,5},{8,10},{9,11},{10,... | collective-permute-start | bytes 786440 | tf_op jit(solution)/shard_map/ppermute | solution.py:155
  60.3 10.7 %collective-permute-start.12 = (bf16[2,128,512]{2,1,0:T(8,128)(2,1)S(1)}, bf16[2,128,512]{2,1,0:T(8,128)(2,1)S(1)}, u32[]{:S(2)}, u32[]{:S(2)}) collective-permute-start(bf16[2,128,512]{2,1,0:T(8,128)(2,1)S(1)} %bitcast.31), channel_id=1, source_target_pairs={{0,2},{1,3},{2,0},{3,1},{4,6},{5,7},{6,4},{7,5},{8,10},{9,11},{10,... | collective-permute-start | bytes 786440 | tf_op jit(solution)/shard_map/ppermute | solution.py:155
  62.1 17.5 %collective-permute-start.15 = (bf16[2,128,512]{2,1,0:T(8,128)(2,1)S(1)}, bf16[2,128,512]{2,1,0:T(8,128)(2,1)S(1)}, u32[]{:S(2)}, u32[]{:S(2)}) collective-permute-start(bf16[2,128,512]{2,1,0:T(8,128)(2,1)S(1)} %add_convert_fusion.1), channel_id=1, source_target_pairs={{0,12},{1,13},{2,14},{3,15},{4,8},{5,9},{6,10},{7,11},{8,4},{9,5},... | collective-permute-start | bytes 786440 | tf_op jit(solution)/shard_map/ppermute | solution.py:155
  68.0 14.7 %collective-permute-start.17 = (bf16[2,128,512]{2,1,0:T(8,128)(2,1)S(1)}, bf16[2,128,512]{2,1,0:T(8,128)(2,1)S(1)}, u32[]{:S(2)}, u32[]{:S(2)}) collective-permute-start(bf16[2,128,512]{2,1,0:T(8,128)(2,1)S(1)} %add_convert_fusion), channel_id=1, source_target_pairs={{0,4},{1,5},{2,6},{3,7},{4,0},{5,1},{6,2},{7,3},{8,12},{9,13},{10,... | collective-permute-start | bytes 786440 | tf_op jit(solution)/shard_map/ppermute | solution.py:155
  82.9 1.6 %collective-permute-start.18 = (f32[128,512]{1,0:T(8,128)S(1)}, f32[128,512]{1,0:T(8,128)S(1)}, u32[]{:S(2)}, u32[]{:S(2)}) collective-permute-start(f32[128,512]{1,0:T(8,128)S(1)} %slice_bitcast_fusion), channel_id=1, source_target_pairs={{0,1},{1,0},{2,3},{3,2},{4,5},{5,4},{6,7},{7,6},{8,9},{9,8},{10,11... | collective-permute-start | bytes 786440 | tf_op jit(solution)/shard_map/ppermute | solution.py:155
